TPU v7x, 1024 devices: a whole 4x8x16 slice. The times are simulated.
1024 devices in a mesh: grp: 16 (over y_hi, x, core), fsdp: 64 (over z, y_lo).
Axes of the slice: x: 4, y: 8 (y_hi: 2, y_lo: 4; y = y_hi * 4 + y_lo), z: 16, core: 2. Of those that a mesh axis runs over, the one named last changes fastest.
Arguments:
- tokens: bfloat16 [262144, 768], P(('grp', 'fsdp')), may hold values from -6 to 6
- send_order: int32 [1024, 256], P(('grp', 'fsdp')), may hold values from 0 to 255, each once within a row
- recv_order: int32 [1024, 256], P(('grp', 'fsdp')), may hold values from 0 to 255, each once within a row
- row_ids: int32 [1024, 256], P(('grp', 'fsdp')), may hold values from 0 to 3, never falling along the last dimension, each value on 1 to 128 neighbouring positions
- frames: int32 [1024, 4], P(('grp', 'fsdp')), may hold values from 0 to 128
- norm_scale: float32 [2, 768], replicated, may hold values from 0.5 to 1.5
- norm_shift: float32 [2, 768], replicated, may hold values from -3 to 3
- qkv_weight: bfloat16 [768, 1152], P('fsdp'), may hold values from -0.21875 to 0.21875
- d_out: bfloat16 [262144, 384], P(('grp', 'fsdp')), may hold values from -6 to 6
Outputs:
- attended: bfloat16 [262144, 384], P(('grp', 'fsdp'))
- grad_tokens: bfloat16 [262144, 768], P(('grp', 'fsdp'))
- grad_weight: float32 [768, 1152], P('fsdp', 'grp')
- grad_scale: float32 [2, 768], replicated
- grad_shift: float32 [2, 768], replicated
All inputs are finite; a program needn't handle non-finite values.
Results may differ from a plain program's by a relative error of at most 0.02.
Values may be sent and summed in bfloat16 or wider, within the bound.
A program may use at most 32 MiB of HBM per device.

v0:
```python
import jax
import jax.numpy as jnp
from jax import lax
from jax.sharding import PartitionSpec as P

HEADS = 6
HEAD_DIM = 64


epsilon = 1e-06


def audio_flags(row_ids, frames):
    position = jnp.arange(row_ids.shape[0], dtype=jnp.int32)
    before = jnp.sum((row_ids[None, :] < row_ids[:, None]).astype(jnp.int32), axis=1)
    place = position - before
    one_hot = row_ids[:, None] == jnp.arange(frames.shape[0], dtype=jnp.int32)[None, :]
    video_limit = jnp.sum(jnp.where(one_hot, frames[None, :], 0), axis=1)
    return place >= video_limit


def shards(
    tokens, send_order, recv_order, row_ids, frames, norm_scale, norm_shift, qkv_weight, d_out
):
    peer_count = lax.axis_size("fsdp")
    slot_count = tokens.shape[0]
    model_width = tokens.shape[1]
    per_peer = slot_count // peer_count
    outgoing = tokens[send_order[0]].reshape(peer_count, per_peer, model_width)
    incoming = lax.all_to_all(outgoing, "fsdp", split_axis=0, concat_axis=0, tiled=True).reshape(
        slot_count, model_width
    )
    packed = incoming[recv_order[0]]
    weight = lax.all_gather(qkv_weight, "fsdp", axis=0, tiled=True)
    values_f32 = packed.astype(jnp.float32)
    average = jnp.mean(values_f32, axis=1, keepdims=True)
    centered = values_f32 - average
    variance = jnp.mean(centered * centered, axis=1, keepdims=True)
    inverse_std = lax.rsqrt(variance + epsilon)
    standard = centered * inverse_std
    is_audio = audio_flags(row_ids[0], frames[0])[:, None]
    row_gain = jnp.where(is_audio, norm_scale[1][None, :], norm_scale[0][None, :])
    row_bias = jnp.where(is_audio, norm_shift[1][None, :], norm_shift[0][None, :])
    normalized = (standard * row_gain + row_bias).astype(jnp.bfloat16)
    qkv = jnp.dot(normalized, weight, preferred_element_type=jnp.float32).astype(jnp.bfloat16)
    inner = HEADS * HEAD_DIM
    query_rows = qkv[:, :inner].reshape(slot_count, HEADS, HEAD_DIM)
    key_rows = qkv[:, inner : 2 * inner].reshape(slot_count, HEADS, HEAD_DIM)
    value_rows = qkv[:, 2 * inner :].reshape(slot_count, HEADS, HEAD_DIM)
    scaling = 1.0 / HEAD_DIM**0.5
    scores = (
        jnp.einsum("qhd,khd->hqk", query_rows, key_rows, preferred_element_type=jnp.float32)
        * scaling
    )
    same_row = (row_ids[0][:, None] == row_ids[0][None, :])[None, :, :]
    scores = jnp.where(same_row, scores, -1e30)
    peak = jnp.max(scores, axis=2, keepdims=True)
    exponent = jnp.exp(scores - peak)
    attn_probs = (exponent / jnp.sum(exponent, axis=2, keepdims=True)).astype(jnp.bfloat16)
    attended = (
        jnp.einsum("hqk,khd->qhd", attn_probs, value_rows, preferred_element_type=jnp.float32)
        .reshape(slot_count, inner)
        .astype(jnp.bfloat16)
    )
    grad_heads = d_out.reshape(slot_count, HEADS, HEAD_DIM)
    grad_probs = jnp.einsum(
        "qhd,khd->hqk", grad_heads, value_rows, preferred_element_type=jnp.float32
    )
    row_delta = jnp.sum(
        grad_heads.astype(jnp.float32)
        * attended.reshape(slot_count, HEADS, HEAD_DIM).astype(jnp.float32),
        axis=2,
    )
    grad_scores = (
        attn_probs.astype(jnp.float32)
        * (grad_probs - jnp.transpose(row_delta)[:, :, None])
        * scaling
    ).astype(jnp.bfloat16)
    grad_query = jnp.einsum(
        "hqk,khd->qhd", grad_scores, key_rows, preferred_element_type=jnp.float32
    ).reshape(slot_count, inner)
    grad_key = jnp.einsum(
        "hqk,qhd->khd", grad_scores, query_rows, preferred_element_type=jnp.float32
    ).reshape(slot_count, inner)
    grad_value = jnp.einsum(
        "hqk,qhd->khd", attn_probs, grad_heads, preferred_element_type=jnp.float32
    ).reshape(slot_count, inner)
    grad_qkv = jnp.concatenate([grad_query, grad_key, grad_value], axis=1).astype(jnp.bfloat16)
    grad_normed = lax.dot_general(
        grad_qkv, weight, (((1,), (1,)), ((), ())), preferred_element_type=jnp.float32
    )
    gain_term = grad_normed * standard
    scale_term = jnp.stack(
        [
            jnp.sum(jnp.where(is_audio, 0.0, gain_term), axis=0),
            jnp.sum(jnp.where(is_audio, gain_term, 0.0), axis=0),
        ]
    )
    shift_term = jnp.stack(
        [
            jnp.sum(jnp.where(is_audio, 0.0, grad_normed), axis=0),
            jnp.sum(jnp.where(is_audio, grad_normed, 0.0), axis=0),
        ]
    )
    scaled = grad_normed * row_gain
    grad_packed = inverse_std * (
        scaled
        - jnp.mean(scaled, axis=1, keepdims=True)
        - standard * jnp.mean(scaled * standard, axis=1, keepdims=True)
    )
    grad_packed = grad_packed.astype(jnp.bfloat16)
    placed = jnp.zeros_like(incoming).at[recv_order[0]].set(grad_packed)
    returned = lax.all_to_all(
        placed.reshape(peer_count, per_peer, model_width),
        "fsdp",
        split_axis=0,
        concat_axis=0,
        tiled=True,
    ).reshape(slot_count, model_width)
    grad_tokens = jnp.zeros_like(tokens).at[send_order[0]].set(returned)
    owned = lax.psum_scatter(
        lax.dot_general(
            normalized, grad_qkv, (((0,), (0,)), ((), ())), preferred_element_type=jnp.float32
        ),
        "fsdp",
        scatter_dimension=0,
        tiled=True,
    )
    grad_weight = lax.psum_scatter(
        owned.astype(jnp.bfloat16), "grp", scatter_dimension=1, tiled=True
    ).astype(jnp.float32)
    grad_scale, grad_shift = lax.psum((scale_term, shift_term), ("grp", "fsdp"))
    return (attended, grad_tokens, grad_weight, grad_scale, grad_shift)


def solution(mesh):
    placed = (
        P(("grp", "fsdp"), None),
        P(("grp", "fsdp"), None),
        P(("grp", "fsdp"), None),
        P(("grp", "fsdp"), None),
        P(("grp", "fsdp"), None),
        P(),
        P(),
        P("fsdp", None),
        P(("grp", "fsdp"), None),
    )
    return jax.shard_map(
        shards,
        mesh=mesh,
        in_specs=placed,
        out_specs=(P(("grp", "fsdp"), None), P(("grp", "fsdp"), None), P("fsdp", "grp"), P(), P()),
        check_vma=False,
    )
```

profile of v0, /device:TPU:1, one launch (start us, length us, event | category | flops | bytes accessed | tf_op | source)
XLA Modules:
  0.0 808.2 jit_solution(15261109821067981632)
XLA Ops:
  11.2 23.4 %all-to-all-start = ((bf16[64,4,768]{2,1,0:T(4,128)(2,1)}), bf16[64,4,768]{2,1,0:T(4,128)(2,1)S(1)}, u32[]{:S(2)}, u32[]{:S(2)}) async-start(bf16[64,4,768]{2,1,0:T(4,128)(2,1)} %reshape.167), calls=%async_computation | async-start | bytes 786432 | tf_op jit(solution)/shard_map/all_to_all | solution.py:30
  35.8 24.3 %all-to-all-done = bf16[64,4,768]{2,1,0:T(4,128)(2,1)S(1)} async-done(((bf16[64,4,768]{2,1,0:T(4,128)(2,1)}), bf16[64,4,768]{2,1,0:T(4,128)(2,1)S(1)}, u32[]{:S(2)}, u32[]{:S(2)}) %all-to-all-start) | async-done | bytes 393248 | tf_op jit(solution)/shard_map/all_to_all | solution.py:30
  61.9 218.4 %all-gather.3.cloned.1.call-done = bf16[64,12,1152]{2,1,0:T(8,128)(2,1)} async-done(((bf16[1,12,1152]{2,1,0:T(8,128)(2,1)}), bf16[64,12,1152]{2,1,0:T(8,128)(2,1)}) %all-gather.3.cloned.1.call-update) | async-done | bytes 1769488 | tf_op jit(solution)/shard_map/all_gather | solution.py:34
  280.3 2.5 reshape.211
  284.2 2.7 fusion.42
  286.9 1.5 divide_convert_fusion
  290.9 1.7 select_reduce_fusion.1
  292.6 2.7 fusion.28
  295.3 2.1 scatter_custom_fusion
  298.3 12.4 %all-to-all-start.1 = ((bf16[64,4,768]{2,1,0:T(4,128)(2,1)}), bf16[64,4,768]{2,1,0:T(4,128)(2,1)S(1)}, u32[]{:S(2)}, u32[]{:S(2)}) async-start(bf16[64,4,768]{2,1,0:T(4,128)(2,1)} %reshape.176), calls=%async_computation.1 | async-start | bytes 786432 | tf_op jit(solution)/shard_map/all_to_all | solution.py:113
  310.7 160.2 %fusion = f32[16,1152]{1,0:T(8,128)S(1)} fusion(f32[768,1152]{1,0:T(8,128)} %fusion.28), kind=kCustom, calls=%all-reduce-scatter | all-reduce-scatter fusion | flops 1179649 | bytes 3616768
  471.0 6.6 collective-permute-start.15
  477.6 7.2 collective-permute-start.14
  484.8 1.3 collective-permute-start.13
  486.1 1.3 collective-permute-start.12
  487.4 1.3 collective-permute-start.11
  488.7 5.3 collective-permute-start.10
  494.0 1.4 dynamic-slice.6
  496.0 1.4 dynamic-slice.2
  498.1 4.8 collective-permute-start.9
  502.9 2.5 collective-permute-start.8
  505.5 1.3 collective-permute-start.7
  506.8 4.9 collective-permute-start.6
  511.7 1.3 collective-permute-start.5
  513.1 1.3 collective-permute-start.4
  514.4 3.4 collective-permute-start.3
  517.8 4.0 collective-permute-start.2
  523.2 2.8 collective-permute-start
  526.8 189.5 %all-reduce.3 = (f32[2,768]{1,0:T(2,128)}, f32[2,768]{1,0:T(2,128)}) all-reduce(f32[2,768]{1,0:T(2,128)S(1)} %pad_maximum_fusion.3, f32[2,768]{1,0:T(2,128)S(1)} %pad_maximum_fusion.4), channel_id=1, replica_groups=mesh['grp'=16,'fsdp'=64] {'grp','fsdp'}, use_global_device_ids=true, to_apply=%region_15.16 | all-reduce | flops 3072 | bytes 24576 | tf_op jit(solution)/shard_map/psum | solution.py:132
  716.4 2.8 concatenate.5
  719.3 78.8 %all-reduce.1 = bf16[12,1152]{1,0:T(8,128)(2,1)S(1)} all-reduce(bf16[12,1152]{1,0:T(8,128)(2,1)S(1)} %dynamic-slice_convert_fusion), channel_id=3, replica_groups=mesh['grp'=16,'fsdp'=64] {'grp'}, use_global_device_ids=true, to_apply=%region_12.13.clone | all-reduce | flops 13824 | bytes 55296
  798.9 2.5 scatter_custom_fusion.1
  (107 shorter events, 14.5 us)
Async XLA Ops:
  7.2 273.1 %all-gather.3.cloned.1.call-start = ((), (), s32[]{:S(2)}) async-start(), calls=%async_computation.2 | async-start | bytes 2396160 | tf_op jit(solution)/shard_map/all_gather | solution.py:34
  10.3 24.4 %copy-start.20 = (s32[1,256]{1,0:T(1,128)S(1)}, s32[1,256]{1,0:T(1,128)}, u32[]{:S(2)}) copy-start(s32[1,256]{1,0:T(1,128)} %param.11) | copy-start | bytes 3076
  10.3 24.5 %copy-start.3 = (s32[1,256]{1,0:T(1,128)S(1)}, s32[1,256]{1,0:T(1,128)}, u32[]{:S(2)}) copy-start(s32[1,256]{1,0:T(1,128)} %param.12) | copy-start | bytes 3076
  10.4 24.5 %copy-start.21 = (s32[1,4]{1,0:T(1,128)S(1)}, s32[1,4]{1,0:T(1,128)}, u32[]{:S(2)}) copy-start(s32[1,4]{1,0:T(1,128)} %param.13) | copy-start | bytes 52
  10.4 24.5 %copy-start.9 = (f32[2,768]{1,0:T(2,128)S(1)}, f32[2,768]{1,0:T(2,128)}, u32[]{:S(2)}) copy-start(f32[2,768]{1,0:T(2,128)} %param.15) | copy-start | bytes 18436
  10.4 24.5 %copy-start.10 = (f32[2,768]{1,0:T(2,128)S(1)}, f32[2,768]{1,0:T(2,128)}, u32[]{:S(2)}) copy-start(f32[2,768]{1,0:T(2,128)} %param.14) | copy-start | bytes 18436
  11.2 48.9 %all-to-all-start = ((bf16[64,4,768]{2,1,0:T(4,128)(2,1)}), bf16[64,4,768]{2,1,0:T(4,128)(2,1)S(1)}, u32[]{:S(2)}, u32[]{:S(2)}) async-start(bf16[64,4,768]{2,1,0:T(4,128)(2,1)} %reshape.167), calls=%async_computation | async-start | bytes 786432 | tf_op jit(solution)/shard_map/all_to_all | solution.py:30
  35.0 247.9 %copy-start.4 = (f32[768]{0:T(1024)}, f32[768]{0:T(1024)S(1)}, u32[]{:S(2)}) copy-start(f32[768]{0:T(1024)S(1)} %get-tuple-element.38) | copy-start | bytes 9220
  35.1 247.8 %copy-start.11 = (pred[256]{0:T(512)(128)(4,1)}, pred[256]{0:T(512)(128)(4,1)S(1)}, u32[]{:S(2)}) copy-start(pred[256]{0:T(512)(128)(4,1)S(1)} %subtract_compare_fusion) | copy-start | bytes 772
  61.8 221.0 %copy-start.6 = (f32[256]{0:T(256)}, f32[256]{0:T(256)S(1)}, u32[]{:S(2)}) copy-start(f32[256]{0:T(256)S(1)} %add_rsqrt_fusion) | copy-start | bytes 3076
  298.3 500.5 %all-to-all-start.1 = ((bf16[64,4,768]{2,1,0:T(4,128)(2,1)}), bf16[64,4,768]{2,1,0:T(4,128)(2,1)S(1)}, u32[]{:S(2)}, u32[]{:S(2)}) async-start(bf16[64,4,768]{2,1,0:T(4,128)(2,1)} %reshape.176), calls=%async_computation.1 | async-start | bytes 786432 | tf_op jit(solution)/shard_map/all_to_all | solution.py:113
  310.7 187.4 %copy-start.17 = (f32[768]{0:T(1024)S(1)}, f32[768]{0:T(1024)}, u32[]{:S(2)}) copy-start(f32[768]{0:T(1024)} %get-tuple-element.33) | copy-start | bytes 9220
  310.7 187.4 %copy-start.16 = (f32[768]{0:T(1024)S(1)}, f32[768]{0:T(1024)}, u32[]{:S(2)}) copy-start(f32[768]{0:T(1024)} %get-tuple-element.34) | copy-start | bytes 9220
  310.7 202.3 %copy-start.15 = (f32[768]{0:T(1024)S(1)}, f32[768]{0:T(1024)}, u32[]{:S(2)}) copy-start(f32[768]{0:T(1024)} %get-tuple-element.30) | copy-start | bytes 9220
  310.7 202.3 %copy-start.14 = (f32[768]{0:T(1024)S(1)}, f32[768]{0:T(1024)}, u32[]{:S(2)}) copy-start(f32[768]{0:T(1024)} %get-tuple-element.29) | copy-start | bytes 9220
  310.7 215.3 %copy-start.1 = (bf16[6,64,256]{2,1,0:T(8,128)(2,1)S(1)}, bf16[6,64,256]{2,1,0:T(8,128)(2,1)}, u32[]{:S(2)}) copy-start(bf16[6,64,256]{2,1,0:T(8,128)(2,1)} %get-tuple-element.62) | copy-start | bytes 589828
  471.0 17.7 %collective-permute-start.15 = (bf16[12,1152]{1,0:T(8,128)(2,1)S(1)}, bf16[12,1152]{1,0:T(8,128)(2,1)S(1)}, u32[]{:S(2)}, u32[]{:S(2)}) collective-permute-start(bf16[12,1152]{1,0:T(8,128)(2,1)S(1)} %slice.35), channel_id=1, source_target_pairs={{0,16},{1,17},{2,18},{3,19},{4,20},{5,21},{6,22},{7,23},{8,24},{9,... | collective-permute-start | bytes 82952
  477.6 20.5 %collective-permute-start.14 = (bf16[16,1152]{1,0:T(8,128)(2,1)S(1)}, bf16[16,1152]{1,0:T(8,128)(2,1)S(1)}, u32[]{:S(2)}, u32[]{:S(2)}) collective-permute-start(bf16[16,1152]{1,0:T(8,128)(2,1)S(1)} %convert.54), channel_id=1, source_target_pairs={{0,15},{1,16},{2,17},{3,18},{4,19},{5,20},{6,21},{7,22},{8,23},{9,... | collective-permute-start | bytes 110600
  484.8 18.2 %collective-permute-start.13 = (bf16[16,1152]{1,0:T(8,128)(2,1)S(1)}, bf16[16,1152]{1,0:T(8,128)(2,1)S(1)}, u32[]{:S(2)}, u32[]{:S(2)}) collective-permute-start(bf16[16,1152]{1,0:T(8,128)(2,1)S(1)} %convert.54), channel_id=1, source_target_pairs={{0,14},{1,15},{2,16},{3,17},{4,18},{5,19},{6,20},{7,21},{8,22},{9,... | collective-permute-start | bytes 110600
  486.1 19.4 %collective-permute-start.12 = (bf16[16,1152]{1,0:T(8,128)(2,1)S(1)}, bf16[16,1152]{1,0:T(8,128)(2,1)S(1)}, u32[]{:S(2)}, u32[]{:S(2)}) collective-permute-start(bf16[16,1152]{1,0:T(8,128)(2,1)S(1)} %convert.54), channel_id=1, source_target_pairs={{0,13},{1,14},{2,15},{3,16},{4,17},{5,18},{6,19},{7,20},{8,21},{9,... | collective-permute-start | bytes 110600
  487.4 19.4 %collective-permute-start.11 = (bf16[16,1152]{1,0:T(8,128)(2,1)S(1)}, bf16[16,1152]{1,0:T(8,128)(2,1)S(1)}, u32[]{:S(2)}, u32[]{:S(2)}) collective-permute-start(bf16[16,1152]{1,0:T(8,128)(2,1)S(1)} %convert.54), channel_id=1, source_target_pairs={{0,12},{1,13},{2,14},{3,15},{4,16},{5,17},{6,18},{7,19},{8,20},{9,... | collective-permute-start | bytes 110600
  488.7 23.0 %collective-permute-start.10 = (bf16[16,1152]{1,0:T(8,128)(2,1)S(1)}, bf16[16,1152]{1,0:T(8,128)(2,1)S(1)}, u32[]{:S(2)}, u32[]{:S(2)}) collective-permute-start(bf16[16,1152]{1,0:T(8,128)(2,1)S(1)} %convert.54), channel_id=1, source_target_pairs={{0,11},{1,12},{2,13},{3,14},{4,15},{5,16},{6,17},{7,18},{8,19},{9,... | collective-permute-start | bytes 110600
  498.1 14.9 %collective-permute-start.9 = (bf16[16,1152]{1,0:T(8,128)(2,1)S(1)}, bf16[16,1152]{1,0:T(8,128)(2,1)S(1)}, u32[]{:S(2)}, u32[]{:S(2)}) collective-permute-start(bf16[16,1152]{1,0:T(8,128)(2,1)S(1)} %convert.54), channel_id=1, source_target_pairs={{0,10},{1,11},{2,12},{3,13},{4,14},{5,15},{6,16},{7,17},{8,18},{9,... | collective-permute-start | bytes 110600
  502.9 11.5 %collective-permute-start.8 = (bf16[16,1152]{1,0:T(8,128)(2,1)S(1)}, bf16[16,1152]{1,0:T(8,128)(2,1)S(1)}, u32[]{:S(2)}, u32[]{:S(2)}) collective-permute-start(bf16[16,1152]{1,0:T(8,128)(2,1)S(1)} %convert.54), channel_id=1, source_target_pairs={{0,9},{1,10},{2,11},{3,12},{4,13},{5,14},{6,15},{7,16},{8,17},{9,1... | collective-permute-start | bytes 110600
  505.5 12.4 %collective-permute-start.7 = (bf16[16,1152]{1,0:T(8,128)(2,1)S(1)}, bf16[16,1152]{1,0:T(8,128)(2,1)S(1)}, u32[]{:S(2)}, u32[]{:S(2)}) collective-permute-start(bf16[16,1152]{1,0:T(8,128)(2,1)S(1)} %convert.54), channel_id=1, source_target_pairs={{0,8},{1,9},{2,10},{3,11},{4,12},{5,13},{6,14},{7,15},{8,16},{9,17... | collective-permute-start | bytes 110600
  506.8 15.1 %collective-permute-start.6 = (bf16[16,1152]{1,0:T(8,128)(2,1)S(1)}, bf16[16,1152]{1,0:T(8,128)(2,1)S(1)}, u32[]{:S(2)}, u32[]{:S(2)}) collective-permute-start(bf16[16,1152]{1,0:T(8,128)(2,1)S(1)} %convert.54), channel_id=1, source_target_pairs={{0,7},{1,8},{2,9},{3,10},{4,11},{5,12},{6,13},{7,14},{8,15},{9,16}... | collective-permute-start | bytes 110600
  511.7 11.5 %collective-permute-start.5 = (bf16[16,1152]{1,0:T(8,128)(2,1)S(1)}, bf16[16,1152]{1,0:T(8,128)(2,1)S(1)}, u32[]{:S(2)}, u32[]{:S(2)}) collective-permute-start(bf16[16,1152]{1,0:T(8,128)(2,1)S(1)} %convert.54), channel_id=1, source_target_pairs={{0,6},{1,7},{2,8},{3,9},{4,10},{5,11},{6,12},{7,13},{8,14},{9,15},... | collective-permute-start | bytes 110600
  513.1 203.3 %collective-permute-start.4 = (bf16[16,1152]{1,0:T(8,128)(2,1)S(1)}, bf16[16,1152]{1,0:T(8,128)(2,1)S(1)}, u32[]{:S(2)}, u32[]{:S(2)}) collective-permute-start(bf16[16,1152]{1,0:T(8,128)(2,1)S(1)} %convert.54), channel_id=1, source_target_pairs={{0,5},{1,6},{2,7},{3,8},{4,9},{5,10},{6,11},{7,12},{8,13},{9,14},{... | collective-permute-start | bytes 110600
  514.4 202.0 %collective-permute-start.3 = (bf16[16,1152]{1,0:T(8,128)(2,1)S(1)}, bf16[16,1152]{1,0:T(8,128)(2,1)S(1)}, u32[]{:S(2)}, u32[]{:S(2)}) collective-permute-start(bf16[16,1152]{1,0:T(8,128)(2,1)S(1)} %convert.54), channel_id=1, source_target_pairs={{0,4},{1,5},{2,6},{3,7},{4,8},{5,9},{6,10},{7,11},{8,12},{9,13},{1... | collective-permute-start | bytes 110600
  517.8 198.5 %collective-permute-start.2 = (bf16[16,1152]{1,0:T(8,128)(2,1)S(1)}, bf16[16,1152]{1,0:T(8,128)(2,1)S(1)}, u32[]{:S(2)}, u32[]{:S(2)}) collective-permute-start(bf16[16,1152]{1,0:T(8,128)(2,1)S(1)} %convert.54), channel_id=1, source_target_pairs={{0,3},{1,4},{2,5},{3,6},{4,7},{5,8},{6,9},{7,10},{8,11},{9,12},{10... | collective-permute-start | bytes 110600
  521.9 194.5 %collective-permute-start.1 = (bf16[16,1152]{1,0:T(8,128)(2,1)S(1)}, bf16[16,1152]{1,0:T(8,128)(2,1)S(1)}, u32[]{:S(2)}, u32[]{:S(2)}) collective-permute-start(bf16[16,1152]{1,0:T(8,128)(2,1)S(1)} %convert.54), channel_id=1, source_target_pairs={{0,2},{1,3},{2,4},{3,5},{4,6},{5,7},{6,8},{7,9},{8,10},{9,11},{10,... | collective-permute-start | bytes 110600
  523.2 193.2 %collective-permute-start = (bf16[16,1152]{1,0:T(8,128)(2,1)S(1)}, bf16[16,1152]{1,0:T(8,128)(2,1)S(1)}, u32[]{:S(2)}, u32[]{:S(2)}) collective-permute-start(bf16[16,1152]{1,0:T(8,128)(2,1)S(1)} %convert.54), channel_id=1, source_target_pairs={{0,1},{1,2},{2,3},{3,4},{4,5},{5,6},{6,7},{7,8},{8,9},{9,10},{10,1... | collective-permute-start | bytes 110600
  (9 other events, 36.2 us)
Sparse Core Ops, SparseCore 0:
  10.7 269.5 all-gather.2
where the time goes:
time: 816 us; the launch traced here: 808 us
  blocking collectives  429 us (53%)
  waiting for transfers between devices  243 us (30%)
  starting transfers between devices  86.3 us (11%)
  local copies, waits for them, and re-layouts  17 us (2%)
  between operations  16.1 us (2%)
  matrix products  10.2 us (1%)
    unnamed x2, blocking collectives  239 us
    all_gather x1, waiting for transfers between devices, shards(): weight = lax.all_gather(qkv_weight, 'fsdp', axis=0, tiled=True)  218 us
    psum x1, blocking collectives, shards(): grad_scale, grad_shift = lax.psum((scale_term, shift_term), ('grp', 'fsdp'))  190 us
    unnamed x16, starting transfers between devices  50.5 us
    all_to_all x1, waiting for transfers between devices, shards(): lax.all_to_all(outgoing, 'fsdp', split_axis=0, concat_axis=0, tiled=True)  24.3 us
    all_to_all x1, starting transfers between devices, shards(): lax.all_to_all(outgoing, 'fsdp', split_axis=0, concat_axis=0, tiled=True)  23.4 us
  transfers between devices with their start and end apart: 19, of which 2 were waited for; matrix products, arithmetic and copies ran while one was open for 21% of the time, Pallas kernels for 0%

commit v1 on v0

v1 whole, which is shorter than its diff:
```python
import functools

import jax
import jax.numpy as jnp
import numpy as np
from jax import lax
from jax.experimental import pallas as pl
from jax.experimental.pallas import tpu as pltpu
from jax.sharding import PartitionSpec as P

HEAD_DIM = 64
EPSILON = 1e-06
MESH = pl.DeviceIdType.MESH
BF16 = jnp.bfloat16
F32 = jnp.float32
ROWS16 = 16
ROWS8 = 8
LANES = 128
CHUNKS = 3


class Sizes:
    def __init__(self, grp, fsdp, slots, width, columns):
        self.yh, self.x, self.c = {16: (2, 4, 2), 4: (1, 2, 2), 8: (2, 2, 2)}[grp]
        self.yl = 4 if fsdp == 64 else 2
        self.z = fsdp // self.yl
        self.zb = 4 if self.z == 16 else 2
        self.za = self.z // self.zb
        self.y = self.yh * self.yl
        self.slots, self.width, self.columns = slots, width, columns
        self.inner = columns // 3
        self.per_peer = slots // fsdp
        self.rows = width // fsdp
        self.half_rows = self.rows // 2
        self.col_block = columns // grp
        self.chip_block = self.col_block * self.c
        self.pieces = self.yh * self.x
        self.chunk = width // CHUNKS
        self.half = width // 2
        self.z_lanes = self.z * self.half_rows


def index_rows(s):
    table = np.full((8, max(s.width, s.yl * LANES, s.slots)), -1, np.int32)
    for j in range(s.width):
        h, r = divmod(j, s.half)
        yl, r = divmod(r, s.z_lanes)
        z, i = divmod(r, s.half_rows)
        table[0, j] = (z * s.yl + yl) * s.rows + h * s.half_rows + i
    for yl in range(s.yl):
        for j in range(s.z_lanes):
            table[1, yl * LANES + j] = yl * s.z_lanes + j
    for yl in range(s.yl):
        for z in range(s.z):
            for r in range(s.per_peer):
                q = (yl * s.z + z) * s.per_peer + r
                table[2, q] = (z * s.yl + yl) * s.per_peer + r
    for yl in range(s.yl):
        for i in range(s.rows):
            table[3, yl * ROWS16 + i] = yl * s.rows + i
    for z in range(s.z):
        for i in range(s.half_rows):
            table[4, z * s.half_rows + i] = z * ROWS8 + i
    return table


def one_hot(count, row):
    ids = lax.broadcasted_iota(jnp.int32, (count, row.shape[1]), 0)
    return jnp.where(ids == row, 1.0, 0.0).astype(BF16)


def mm(a, b, dims=((1,), (0,))):
    return lax.dot_general(a, b, (dims, ((), ())), preferred_element_type=F32)


TN = ((0,), (0,))
NT = ((1,), (1,))


def kernel(
    s, tok, send_order, recv_order, row_ids, frames, gains, biases, wshard, dout, table,
    attended, grad_tokens, grad_weight, grad_scale, grad_shift,
    pt, perm, rt, feat, a_out, a_in, b_out, b_in, packed, wpad, wsh, wyin, weight,
    aud, standard, inv, normed, normed_p, qkv, gqkv, gnorm, gpacked,
    r_out, r_in, t_out, t_in, g_send, g_own, g_in, x_out, x_in, y_out, y_in, z_out, z_in,
    f_send, f_in, n_c, n_x, n_y, n_zb, n_za,
    ya_s, ya_r, za_s, za_r, yb_s, yb_r, zb_s, zb_r,
    wz_s, wz_r, wy_s, wy_r, wx_s, wx_r, wc_s, wc_r,
    gc_s, gc_r, gx_s, gx_r, gy_s, gy_r, gz_s, gz_r, gf_s, gf_r,
    nc_s, nc_r, nx_s, nx_r, ny_s, ny_r, nzb_s, nzb_r, nza_s, nza_r,
):
    g = lax.axis_index("grp")
    f = lax.axis_index("fsdp")
    core = g % s.c
    my_x = (g // s.c) % s.x
    my_yh = g // (s.c * s.x)
    my_z = f // s.yl
    my_yl = f % s.yl
    my_y = my_yh * s.yl + my_yl
    other = 1 - core

    def grp_of(yh, x, c):
        return (yh * s.x + x) * s.c + c

    def at_z(z):
        return (g, z * s.yl + my_yl)

    def at_yl(yl):
        return (g, my_z * s.yl + yl)

    def at_y(y):
        return (grp_of(y // s.yl, my_x, core), my_z * s.yl + y % s.yl)

    def at_x(x):
        return (grp_of(my_yh, x, core), f)

    sibling = (grp_of(my_yh, my_x, other), f)

    def others(count, me, body):
        def step(k, carry):
            body((me + k) % count)
            return carry

        lax.fori_loop(1, count, step, 0)

    def remote(src, dst, send, recv, device):
        return pltpu.make_async_remote_copy(
            src_ref=src, dst_ref=dst, send_sem=send, recv_sem=recv,
            device_id=device, device_id_type=MESH,
        )

    barrier = pltpu.get_barrier_semaphore()

    def greet(device):
        pl.semaphore_signal(barrier, inc=1, device_id=device, device_id_type=MESH)

    others(s.z, my_z, lambda z: greet(at_z(z)))
    others(s.y, my_y, lambda y: greet(at_y(y)))
    others(s.x, my_x, lambda x: greet(at_x(x)))
    greet(sibling)

    to_q = one_hot(s.slots, table[2:3, : s.slots])
    perm[...] = to_q
    pt[...] = mm(one_hot(s.slots, send_order[...]), to_q).astype(BF16)
    rt[...] = one_hot(s.slots, recv_order[...])
    wpad[...] = jnp.zeros_like(wpad)
    wpad[0 : s.rows, :] = wshard[...]
    for c in range(CHUNKS):
        a_out[c] = mm(pt[...], tok[:, c * s.chunk : (c + 1) * s.chunk], TN).astype(BF16)
    pl.semaphore_wait(barrier, (s.z - 1) + (s.y - 1) + (s.x - 1) + 1)

    @pl.when(my_z == g)
    def _():
        def send(z):
            remote(wpad, wsh, wz_s.at[z], wz_r.at[0], at_z(z)).start()

        others(s.z, my_z, send)
        wsh[...] = wpad[...]

    run = s.slots // s.yl
    block = s.slots // s.z

    def q_rows(yl):
        return pl.ds(pl.multiple_of(yl * run, run), run)

    def s_rows(z):
        return pl.ds(pl.multiple_of(z * block, block), block)

    def y_copy(out, into, send, recv, c, yl, slot):
        return remote(
            out.at[c, q_rows(yl), :], into.at[c, q_rows(slot), :],
            send.at[c * s.yl + yl], recv.at[c * s.yl + slot], at_yl(yl),
        )

    def z_copy(out, into, send, recv, c, z, slot):
        return remote(
            out.at[c, s_rows(z), :], into.at[c, s_rows(slot), :],
            send.at[c * s.z + z], recv.at[c * s.z + slot], at_z(z),
        )

    def y_start(out, into, send, recv, c):
        others(s.yl, my_yl, lambda y: y_copy(out, into, send, recv, c, y, my_yl).start())
        into[c, q_rows(my_yl), :] = out[c, q_rows(my_yl), :]

    def y_wait(out, into, send, recv, c):
        others(s.yl, my_yl, lambda y: y_copy(out, into, send, recv, c, y, y).wait_recv())

    def z_start(out, into, send, recv, c):
        others(s.z, my_z, lambda z: z_copy(out, into, send, recv, c, z, my_z).start())
        into[c, s_rows(my_z), :] = out[c, s_rows(my_z), :]

    def z_wait(out, into, send, recv, c):
        others(s.z, my_z, lambda z: z_copy(out, into, send, recv, c, z, z).wait_recv())

    first_y = (a_out, a_in, ya_s, ya_r)
    first_z = (b_out, b_in, za_s, za_r)
    back_z = (r_out, r_in, zb_s, zb_r)
    back_y = (t_out, t_in, yb_s, yb_r)
    for c in range(CHUNKS):
        y_start(*first_y, c)

    @pl.when(my_z != g)
    def _():
        remote(wpad, wsh, wz_s.at[0], wz_r.at[0], at_z((my_z + 1) % s.z)).wait_recv()

    def wy_slot(y):
        return wyin.at[y // s.yl, pl.ds(pl.multiple_of((y % s.yl) * ROWS16, ROWS16), ROWS16), :]

    others(s.y, my_y, lambda y: remote(wsh, wy_slot(my_y), wy_s.at[y], wy_r.at[my_y], at_y(y)).start())
    wyin[my_yh, pl.ds(pl.multiple_of(my_yl * ROWS16, ROWS16), ROWS16), :] = wsh[...]

    def first_turn(c):
        y_wait(*first_y, c)
        b_out[c] = mm(perm[...], a_in[c]).astype(BF16)
        z_start(*first_z, c)

    first_turn(0)

    others(s.y, my_y, lambda y: remote(wsh, wy_slot(y), wy_s.at[y], wy_r.at[y], at_y(y)).wait_recv())
    wide = s.yl * s.rows
    pick = one_hot(wide, table[3:4, : s.yl * ROWS16])

    def w_rows(yh, x, c):
        return weight.at[pl.ds(pl.multiple_of(grp_of(yh, x, c) * wide, wide), wide), :]

    for yh in range(s.yh):
        w_rows(yh, my_x, core)[...] = mm(pick, wyin[yh]).astype(BF16)

    def wx_copy(yh, x, slot):
        rows = w_rows(yh, slot, core)
        return remote(rows, rows, wx_s.at[x * s.yh + yh], wx_r.at[slot * s.yh + yh], at_x(x))

    def wc_copy(yh, x, c):
        rows = w_rows(yh, x, c)
        return remote(rows, rows, wc_s.at[x * s.yh + yh], wc_r.at[x * s.yh + yh], sibling)

    for yh in range(s.yh):
        others(s.x, my_x, lambda x, yh=yh: wx_copy(yh, x, my_x).start())
        wc_copy(yh, my_x, core).start()

    for c in range(1, CHUNKS):
        first_turn(c)

    feat[...] = one_hot(s.width, table[0:1, : s.width])
    ids = row_ids[...].astype(F32)
    down = lax.broadcasted_iota(jnp.int32, (s.slots, s.slots), 0)
    across = lax.broadcasted_iota(jnp.int32, (s.slots, s.slots), 1)
    id_col = jnp.sum(jnp.where(down == across, ids, 0.0), axis=1, keepdims=True)
    before = jnp.sum(jnp.where(ids < id_col, 1.0, 0.0), axis=1, keepdims=True)
    place = lax.broadcasted_iota(jnp.int32, (s.slots, 1), 0).astype(F32) - before
    limit = jnp.zeros((s.slots, 1), F32)
    for k in range(frames.shape[1]):
        limit = limit + jnp.where(id_col == k, frames[0:1, k : k + 1].astype(F32), 0.0)
    aud[...] = jnp.where(place >= limit, 1.0, 0.0)

    for x_step in range(1, s.x):
        x = (my_x + x_step) % s.x
        for yh in range(s.yh):
            wx_copy(yh, x, x).wait_recv()
            wc_copy(yh, x, core).start()

    for c in range(CHUNKS):
        z_wait(*first_z, c)
        packed[:, c * s.chunk : (c + 1) * s.chunk] = mm(rt[...], b_in[c], TN).astype(BF16)

    step_rows = 32

    def by_rows(body):
        def step(i, carry):
            body(pl.ds(pl.multiple_of(i * step_rows, step_rows), step_rows))
            return carry

        lax.fori_loop(0, s.slots // step_rows, step, 0)

    def norm(rows):
        values = packed[rows, :].astype(F32)
        centered = values - jnp.mean(values, axis=1, keepdims=True)
        variance = jnp.mean(centered * centered, axis=1, keepdims=True)
        inverse = lax.rsqrt(variance + EPSILON)
        unit = centered * inverse
        inv[rows, :] = inverse
        standard[rows, :] = unit
        audio = jnp.broadcast_to(aud[rows, :], unit.shape) > 0.5
        gain = jnp.where(audio, gains[1:2, :], gains[0:1, :])
        bias = jnp.where(audio, biases[1:2, :], biases[0:1, :])
        normed[rows, :] = (unit * gain + bias).astype(BF16)

    by_rows(norm)
    for h in range(2):
        normed_p[h] = mm(normed[...], feat[:, h * s.half : (h + 1) * s.half]).astype(BF16)

    def wc_all(body):
        for x in range(s.x):
            for yh in range(s.yh):
                body(wc_copy(yh, x, other))

    wc_all(lambda copy: copy.wait_recv())

    def project(i, carry):
        cols = pl.ds(pl.multiple_of(i * s.inner, LANES), s.inner)
        qkv[:, cols] = mm(normed[...], weight[:, cols]).astype(BF16)
        return carry

    lax.fori_loop(0, 3, project, 0)

    pair = 2 * HEAD_DIM
    scaling = 1.0 / HEAD_DIM**0.5

    def heads(i, carry):
        def part(k):
            return pl.ds(pl.multiple_of(k * s.inner + i * pair, LANES), pair)

        lane = lax.broadcasted_iota(jnp.int32, (1, pair), 1)
        masks = [jnp.where(lane < HEAD_DIM, 1.0, 0.0), jnp.where(lane < HEAD_DIM, 0.0, 1.0)]
        row_of = lax.broadcasted_iota(jnp.int32, (s.slots, s.slots), 0)
        col_of = lax.broadcasted_iota(jnp.int32, (s.slots, s.slots), 1)
        ids_row = row_ids[...].astype(F32)
        ids_col = jnp.sum(jnp.where(row_of == col_of, ids_row, 0.0), axis=1, keepdims=True)
        same = ids_row == ids_col
        q, k, v, do = qkv[:, part(0)], qkv[:, part(1)], qkv[:, part(2)], dout[:, part(0)]

        def split(a):
            return [a * m.astype(BF16) for m in masks]

        qs, ks, vs, dos = split(q), split(k), split(v), split(do)
        probs = []
        for a in range(2):
            scores = jnp.where(same, mm(qs[a], k, NT) * scaling, -1e30)
            exponent = jnp.exp(scores - jnp.max(scores, axis=1, keepdims=True))
            probs.append((exponent / jnp.sum(exponent, axis=1, keepdims=True)).astype(BF16))
        out = mm(jnp.concatenate(probs, axis=1), jnp.concatenate(vs, axis=0)).astype(BF16)
        attended[:, part(0)] = out
        delta = do.astype(F32) * out.astype(F32)
        grads = []
        for a in range(2):
            row_delta = jnp.sum(delta * masks[a], axis=1, keepdims=True)
            grad_probs = mm(dos[a], v, NT)
            grads.append((probs[a].astype(F32) * (grad_probs - row_delta) * scaling).astype(BF16))
        gqkv[:, part(0)] = mm(
            jnp.concatenate(grads, axis=1), jnp.concatenate(ks, axis=0)
        ).astype(BF16)
        gqkv[:, part(1)] = mm(
            jnp.concatenate(grads, axis=0), jnp.concatenate(qs, axis=0), TN
        ).astype(BF16)
        gqkv[:, part(2)] = mm(
            jnp.concatenate(probs, axis=0), jnp.concatenate(dos, axis=0), TN
        ).astype(BF16)
        return carry

    lax.fori_loop(0, s.inner // pair, heads, 0)

    def unproject(i, carry):
        rows = pl.ds(pl.multiple_of(i * s.chunk, s.chunk), s.chunk)
        gnorm[i] = mm(gqkv[...], weight[rows, :], NT)
        return carry

    lax.fori_loop(0, CHUNKS, unproject, 0)
    n_c[core] = jnp.zeros_like(n_c[0])

    def unnorm(rows):
        grad = jnp.concatenate([gnorm[c, rows, :] for c in range(CHUNKS)], axis=1)
        unit = standard[rows, :]
        audio = jnp.broadcast_to(aud[rows, :], unit.shape) > 0.5
        gain = jnp.where(audio, gains[1:2, :], gains[0:1, :])
        gain_term = grad * unit
        n_c[core] += jnp.concatenate(
            [
                jnp.sum(jnp.where(audio, 0.0, gain_term), axis=0, keepdims=True),
                jnp.sum(jnp.where(audio, gain_term, 0.0), axis=0, keepdims=True),
                jnp.sum(jnp.where(audio, 0.0, grad), axis=0, keepdims=True),
                jnp.sum(jnp.where(audio, grad, 0.0), axis=0, keepdims=True),
            ],
            axis=0,
        )
        scaled = grad * gain
        out = inv[rows, :] * (
            scaled
            - jnp.mean(scaled, axis=1, keepdims=True)
            - unit * jnp.mean(scaled * unit, axis=1, keepdims=True)
        )
        gpacked[rows, :] = out.astype(BF16)

    by_rows(unnorm)
    for c in range(CHUNKS):
        r_out[c] = mm(rt[...], gpacked[:, c * s.chunk : (c + 1) * s.chunk]).astype(BF16)
        z_start(*back_z, c)

    third = s.columns // 3

    def third_rows(k):
        return pl.ds(pl.multiple_of(k * third, third), third)

    def gc_copy(k):
        return remote(g_send.at[third_rows(k), :], g_in.at[third_rows(k), :], gc_s.at[k], gc_r.at[k], sibling)

    for k in range(3):
        g_send[third_rows(k), :] = mm(gqkv[:, k * third : (k + 1) * third], normed_p[other], TN).astype(BF16)
        gc_copy(k).start()

    def n_copy(buf, slot, peer, send, recv, device):
        return remote(buf.at[slot], buf.at[slot], send.at[peer], recv.at[slot], device)

    n_copy(n_c, core, other, nc_s, nc_r, sibling).start()

    for k in range(3):
        g_own[third_rows(k), :] = mm(gqkv[:, k * third : (k + 1) * third], normed_p[core], TN)

    def total(buf, count):
        result = buf[0]
        for k in range(1, count):
            result = result + buf[k]
        return result

    def n_start(buf, count, me, send, recv, at, value):
        buf[me] = value
        others(count, me, lambda p: n_copy(buf, me, p, send, recv, at(p)).start())

    def n_wait(buf, count, me, send, recv, at):
        others(count, me, lambda p: n_copy(buf, p, p, send, recv, at(p)).wait_recv())

    by_x = (n_x, s.x, my_x, nx_s, nx_r, at_x)
    by_y = (n_y, s.y, my_y, ny_s, ny_r, at_y)
    my_za, my_zb = my_z // s.zb, my_z % s.zb
    by_zb = (n_zb, s.zb, my_zb, nzb_s, nzb_r, lambda zb: at_z(my_za * s.zb + zb))
    by_za = (n_za, s.za, my_za, nza_s, nza_r, lambda za: at_z(za * s.zb + my_zb))

    n_copy(n_c, other, other, nc_s, nc_r, sibling).wait_recv()
    n_start(*by_x, total(n_c, s.c))

    def piece_rows(p):
        return pl.ds(pl.multiple_of(p * s.chip_block, ROWS16), s.chip_block)

    def gx_copy(yh, x, slot):
        return remote(
            x_out.at[piece_rows(yh * s.x + x), :], x_in.at[slot, yh],
            gx_s.at[x * s.yh + yh], gx_r.at[slot * s.yh + yh], at_x(x),
        )

    sent = 0
    for k in range(3):
        gc_copy(k).wait_recv()
        both = g_own[third_rows(k), :] + g_in[third_rows(k), :].astype(F32)
        g_own[third_rows(k), :] = both
        x_out[third_rows(k), :] = both.astype(BF16)
        while (sent + 1) * s.chip_block <= (k + 1) * third:
            yh, x = sent // s.x, sent % s.x

            @pl.when(x != my_x)
            def _(yh=yh, x=x):
                gx_copy(yh, x, my_x).start()

            sent += 1

    def back_turn(c):
        z_wait(*back_z, c)
        t_out[c] = mm(perm[...], r_in[c], TN).astype(BF16)
        y_start(*back_y, c)

    back_turn(0)
    n_wait(*by_x)
    n_start(*by_y, total(n_x, s.x))
    back_turn(1)

    spread = one_hot(s.half, table[1:2, : s.yl * LANES])
    for yh in range(s.yh):
        others(s.x, my_x, lambda x, yh=yh: gx_copy(yh, x, x).wait_recv())
        piece = g_own[piece_rows(yh * s.x + my_x), :]
        for step in range(1, s.x):
            piece = piece + x_in[(my_x + step) % s.x, yh].astype(F32)
        wide_piece = mm(piece.astype(BF16), spread).astype(BF16)
        for yl in range(s.yl):
            y_out[yh * s.yl + yl] = wide_piece[:, yl * LANES : (yl + 1) * LANES]
    others(s.y, my_y, lambda y: remote(y_out.at[y], y_in.at[my_y], gy_s.at[y], gy_r.at[my_y], at_y(y)).start())
    y_in[my_y] = y_out[my_y]

    n_wait(*by_y)
    n_start(*by_zb, total(n_y, s.y))
    back_turn(2)

    others(s.y, my_y, lambda y: remote(y_out.at[y], y_in.at[y], gy_s.at[y], gy_r.at[y], at_y(y)).wait_recv())
    piece = y_in[0].astype(F32)
    for y in range(1, s.y):
        piece = piece + y_in[y].astype(F32)
    apart = one_hot(s.z * ROWS8, table[4:5, :LANES])
    z_out[...] = mm(apart, piece.astype(BF16), NT)

    def z_tile(z):
        return z_out.at[pl.ds(pl.multiple_of(z * ROWS8, ROWS8), ROWS8), :]

    others(s.z, my_z, lambda z: remote(z_tile(z), z_in.at[my_z], gz_s.at[z], gz_r.at[my_z], at_z(z)).start())
    z_in[my_z] = z_out[pl.ds(pl.multiple_of(my_z * ROWS8, ROWS8), ROWS8), :]

    n_wait(*by_zb)
    n_start(*by_za, total(n_zb, s.zb))

    def home(c):
        y_wait(*back_y, c)
        grad_tokens[:, c * s.chunk : (c + 1) * s.chunk] = mm(pt[...], t_in[c]).astype(BF16)

    home(0)
    home(1)
    others(s.z, my_z, lambda z: remote(z_tile(z), z_in.at[z], gz_s.at[z], gz_r.at[z], at_z(z)).wait_recv())
    own = total(z_in, s.z)
    f_send[...] = own
    f_copy = remote(f_send, f_in, gf_s.at[0], gf_r.at[0], sibling)
    f_copy.start()
    home(2)
    n_wait(*by_za)
    norms = total(n_za, s.za)
    grad_scale[...] = norms[0:2]
    grad_shift[...] = norms[2:4]
    f_copy.wait_recv()
    first = core == 0
    theirs = f_in[...]
    low, high = jnp.where(first, own, theirs), jnp.where(first, theirs, own)
    for part, (at, value) in enumerate(((0, low), (s.half_rows, high))):
        mine = jnp.where(first, value[:, : s.col_block], value[:, s.col_block :])
        grad_weight[at : at + s.half_rows, :] = mine[: s.half_rows]

    @pl.when(my_z == g)
    def _():
        others(s.z, my_z, lambda z: remote(wpad, wsh, wz_s.at[z], wz_r.at[0], at_z(z)).wait_send())

    for c in range(CHUNKS):
        for way in (first_y, back_y):
            others(s.yl, my_yl, lambda y: y_copy(*way, c, y, my_yl).wait_send())
        for way in (first_z, back_z):
            others(s.z, my_z, lambda z: z_copy(*way, c, z, my_z).wait_send())
    others(s.y, my_y, lambda y: remote(wsh, wy_slot(my_y), wy_s.at[y], wy_r.at[my_y], at_y(y)).wait_send())
    for yh in range(s.yh):
        others(s.x, my_x, lambda x, yh=yh: wx_copy(yh, x, my_x).wait_send())
        others(s.x, my_x, lambda x, yh=yh: gx_copy(yh, x, my_x).wait_send())
    wc_all(lambda copy: copy.wait_send())
    for k in range(3):
        gc_copy(k).wait_send()
    others(s.y, my_y, lambda y: remote(y_out.at[y], y_in.at[my_y], gy_s.at[y], gy_r.at[my_y], at_y(y)).wait_send())
    others(s.z, my_z, lambda z: remote(z_tile(z), z_in.at[my_z], gz_s.at[z], gz_r.at[my_z], at_z(z)).wait_send())
    f_copy.wait_send()
    n_copy(n_c, core, other, nc_s, nc_r, sibling).wait_send()
    for buf, count, me, send, recv, at in (by_x, by_y, by_zb, by_za):
        others(count, me, lambda p: n_copy(buf, me, p, send, recv, at(p)).wait_send())


def shards(
    tokens, send_order, recv_order, row_ids, frames, norm_scale, norm_shift, qkv_weight, d_out
):
    slots, width = tokens.shape
    columns = qkv_weight.shape[1]
    s = Sizes(lax.axis_size("grp"), lax.axis_size("fsdp"), slots, width, columns)
    whole = pl.BlockSpec(memory_space=pltpu.VMEM)
    vm, dma = pltpu.VMEM, pltpu.SemaphoreType.DMA
    moved = vm((CHUNKS, slots, s.chunk), BF16)
    norms = (4, width)
    scratch = [
        vm((slots, slots), BF16), vm((slots, slots), BF16), vm((slots, slots), BF16),
        vm((width, width), BF16), moved, moved, moved, moved, vm((slots, width), BF16),
        vm((ROWS16, columns), BF16), vm((ROWS16, columns), BF16),
        vm((s.yh, s.yl * ROWS16, columns), BF16), vm((width, columns), BF16),
        vm((slots, 1), F32), vm((slots, width), F32), vm((slots, 1), F32),
        vm((slots, width), BF16), vm((2, slots, s.half), BF16),
        vm((slots, columns), BF16), vm((slots, columns), BF16),
        vm((CHUNKS, slots, s.chunk), F32), vm((slots, width), BF16),
        moved, moved, moved, moved,
        vm((columns, s.half), BF16), vm((columns, s.half), F32), vm((columns, s.half), BF16),
        vm((columns, s.half), BF16), vm((s.x, s.yh, s.chip_block, s.half), BF16),
        vm((s.y, s.chip_block, LANES), BF16), vm((s.y, s.chip_block, LANES), BF16),
        vm((s.z * ROWS8, s.chip_block), F32), vm((s.z, ROWS8, s.chip_block), F32),
        vm((ROWS8, s.chip_block), F32), vm((ROWS8, s.chip_block), F32),
        vm((s.c,) + norms, F32), vm((s.x,) + norms, F32), vm((s.y,) + norms, F32),
        vm((s.zb,) + norms, F32), vm((s.za,) + norms, F32),
    ]
    y3, z3 = CHUNKS * s.yl, CHUNKS * s.z
    xy = s.x * s.yh
    counts = [y3, y3, z3, z3, y3, y3, z3, z3]
    counts += [s.z, 1, s.y, s.y, xy, xy, xy, xy]
    counts += [3, 3, xy, xy, s.y, s.y, s.z, s.z, 1, 1]
    counts += [s.c, s.c, s.x, s.x, s.y, s.y, s.zb, s.zb, s.za, s.za]
    scratch += [dma((n,)) for n in counts]
    sds = jax.ShapeDtypeStruct
    return pl.pallas_call(
        functools.partial(kernel, s),
        out_shape=(
            sds((slots, s.inner), BF16), sds((slots, width), BF16),
            sds((s.rows, s.col_block), F32), sds((2, width), F32), sds((2, width), F32),
        ),
        in_specs=[whole] * 10,
        out_specs=(whole,) * 5,
        scratch_shapes=scratch,
        compiler_params=pltpu.CompilerParams(
            collective_id=0, has_side_effects=True, vmem_limit_bytes=56 * 1024 * 1024
        ),
        cost_estimate=pl.CostEstimate(
            flops=2_000_000_000, bytes_accessed=3_000_000, transcendentals=400_000
        ),
        name="joint_block",
    )(
        tokens, send_order, recv_order, row_ids, frames, norm_scale, norm_shift, qkv_weight, d_out,
        jnp.asarray(index_rows(s)),
    )


def solution(mesh):
    rows = P(("grp", "fsdp"), None)
    return jax.shard_map(
        shards,
        mesh=mesh,
        in_specs=(rows, rows, rows, rows, rows, P(), P(), P("fsdp", None), rows),
        out_specs=(rows, rows, P("fsdp", "grp"), P(), P()),
        check_vma=False,
    )
```

time: 816 us -> 120 us (0.15)
  blocking collectives: 429 us -> 0 us
  waiting for transfers between devices: 243 us -> 0 us
  Pallas kernels: 0 us -> 113 us
  starting transfers between devices: 86.3 us -> 0 us
  between operations: 16.1 us -> 0.66 us
  local copies, waits for them, and re-layouts: 17 us -> 4.41 us
  matrix products: 10.2 us -> 0 us
    unnamed x2 -> x0, blocking collectives: 239 us -> none
    all_gather x1 -> x0, waiting for transfers between devices: 218 us -> none  [shards(): weight = lax.all_gather(qkv_weight, 'fsdp', axis=0, tiled=True)]
    psum x1 -> x0, blocking collectives: 190 us -> none  [shards(): grad_scale, grad_shift = lax.psum((scale_term, shift_term), ('grp', 'fsdp'))]
    pallas_call x0 -> x1, Pallas kernels: none -> 113 us  [shards(): pl.pallas_call(functools.partial(kernel, s), out_shape=(sds((slots, s.inn...]
    unnamed x16 -> x0, starting transfers between devices: 50.5 us -> none
    all_to_all x2 -> x0, starting transfers between devices: 35.8 us -> none  [the longest x1 23.4 us: shards(): lax.all_to_all(outgoing, 'fsdp', split_axis=0, concat_axis=0, tiled=True)]
    all_to_all x2 -> x0, waiting for transfers between devices: 24.3 us -> none  [the longest x1 24.3 us: shards(): lax.all_to_all(outgoing, 'fsdp', split_axis=0, concat_axis=0, tiled=True)]
  transfers between devices with their start and end apart: 19 -> 0, of which waited for: 2 -> 0; matrix products, arithmetic and copies ran while one was open for 21% -> 0% of each run, Pallas kernels for 0% -> 0%
where the time goes in v1:
time: 120 us; the launch traced here: 119 us
  Pallas kernels  113 us (94%)
  local copies, waits for them, and re-layouts  4.41 us (4%)
    pallas_call x1, Pallas kernels, shards(): pl.pallas_call(functools.partial(kernel, s), out_shape=(sds((slots, s.inn...  113 us
    unnamed x13, local copies, waits for them, and re-layouts  4.41 us

profile of v1, /device:TPU:1, one launch (start us, length us, event | category | flops | bytes accessed | tf_op | source)
XLA Modules:
  0.0 118.5 jit_solution(1924159755034003660)
XLA Ops:
  0.6 113.5 %joint_block.1 = (bf16[256,384]{1,0:T(8,128)(2,1)}, bf16[256,768]{1,0:T(8,128)(2,1)}, f32[12,72]{1,0:T(8,128)}, f32[2,768]{1,0:T(2,128)}, f32[2,768]{1,0:T(2,128)}) custom-call(bf16[256,768]{1,0:T(8,128)(2,1)} %tok.1, s32[1,256]{1,0:T(1,128)} %send_order.1, s32[1,256]{1,0:T(1,128)} %recv_order.1, s32[1,256]{1,0:T(1,128)} %row_ids.1, s32[1,4]{1,0:T(1,128)} %frames.1, ...), custom_call_target="tpu_custom_call" | custom-call | flops 2000000000 | bytes 3000000 | tf_op jit(solution)/shard_map/joint_block/pallas_call | solution.py:580
  114.1 0.0 copy-start
  114.1 1.7 %copy.20 = bf16[256,384]{1,0:T(8,128)(2,1)} copy(bf16[256,384]{1,0:T(8,128)(2,1)} %get-tuple-element.10) | data formatting | bytes 393216
  115.8 0.0 copy-done
  115.8 0.0 copy-start.1
  115.8 0.7 copy.21
  116.5 0.0 copy-done.1
  116.5 0.0 copy-start.3
  116.5 0.6 copy.22
  117.1 0.1 copy-done.3
  117.2 0.0 copy-start.2
  117.2 0.6 copy.23
  117.8 0.1 copy-done.2
  117.9 0.6 copy.24
Async XLA Ops:
  114.1 1.7 %copy-start = (bf16[256,768]{1,0:T(8,128)(2,1)S(1)}, bf16[256,768]{1,0:T(8,128)(2,1)}, u32[]{:S(2)}) copy-start(bf16[256,768]{1,0:T(8,128)(2,1)} %get-tuple-element.11) | copy-start | bytes 1179652
  115.8 0.8 copy-start.1
  116.5 0.7 copy-start.3
  117.2 0.7 copy-start.2

commit v2 on v1

v2 whole, which is shorter than its diff:
```python
import functools

import jax
import jax.numpy as jnp
import numpy as np
from jax import lax
from jax.experimental import pallas as pl
from jax.experimental.pallas import tpu as pltpu
from jax.sharding import PartitionSpec as P

HEAD_DIM = 64
EPSILON = 1e-06
MESH = pl.DeviceIdType.MESH
BF16 = jnp.bfloat16
F32 = jnp.float32
ROWS16 = 16
ROWS8 = 8
LANES = 128
CHUNKS = 3
NORM_ROWS = 64
UNNORM_ROWS = 64


class Sizes:
    def __init__(self, grp, fsdp, slots, width, columns):
        self.yh, self.x, self.c = {16: (2, 4, 2), 4: (1, 2, 2), 8: (2, 2, 2)}[grp]
        self.yl = 4 if fsdp == 64 else 2
        self.z = fsdp // self.yl
        self.zb = 4 if self.z == 16 else 2
        self.za = self.z // self.zb
        self.y = self.yh * self.yl
        self.slots, self.width, self.columns = slots, width, columns
        self.inner = columns // 3
        self.per_peer = slots // fsdp
        self.rows = width // fsdp
        self.half_rows = self.rows // 2
        self.col_block = columns // grp
        self.chip_block = self.col_block * self.c
        self.pieces = self.yh * self.x
        self.chunk = width // CHUNKS
        self.half = width // 2
        self.z_lanes = self.z * self.half_rows
        self.fold = (columns // LANES * 2 // 9) * LANES
        self.kept = columns - self.fold


def index_rows(s):
    table = np.full((8, max(s.width, s.yl * LANES, s.slots)), -1, np.int32)
    for j in range(s.width):
        h, r = divmod(j, s.half)
        yl, r = divmod(r, s.z_lanes)
        z, i = divmod(r, s.half_rows)
        table[0, j] = (z * s.yl + yl) * s.rows + h * s.half_rows + i
    for yl in range(s.yl):
        for j in range(s.z_lanes):
            table[1, yl * LANES + j] = yl * s.z_lanes + j
    for yl in range(s.yl):
        for z in range(s.z):
            for r in range(s.per_peer):
                q = (yl * s.z + z) * s.per_peer + r
                table[2, q] = (z * s.yl + yl) * s.per_peer + r
    for yl in range(s.yl):
        for i in range(s.rows):
            table[3, yl * ROWS16 + i] = yl * s.rows + i
            table[5 + i % 3, yl * ROWS16 + s.rows + i // 3] = yl * s.rows + i
    for z in range(s.z):
        for i in range(s.half_rows):
            table[4, z * s.half_rows + i] = z * ROWS8 + i
    return table


def one_hot(count, row):
    ids = lax.broadcasted_iota(jnp.int32, (count, row.shape[1]), 0)
    return jnp.where(ids == row, 1.0, 0.0).astype(BF16)


def mm(a, b, dims=((1,), (0,))):
    return lax.dot_general(a, b, (dims, ((), ())), preferred_element_type=F32)


TN = ((0,), (0,))
NT = ((1,), (1,))


def kernel(
    s, tok_h, send_order_h, recv_order_h, row_ids_h, frames_h, gains_h, biases_h, wshard_h, dout_h, table_h,
    attended_h, grad_tokens_h, grad_weight_h, grad_scale_h, grad_shift_h,
    tok, send_order, recv_order, row_ids, frames, gains, biases, wshard, dout, table,
    attended, grad_tokens, grad_weight, grad_scale, grad_shift,
    pt, pt_q, perm, rt, rt_q, feat, a_out, a_in, b_out, b_in, packed, wpad, wsh, wyin, weight,
    aud, same, standard, inv, normed, normed_p, qkv, gqkv, gnorm, gpacked,
    r_out, r_in, t_out, t_in, g_send, g_own, g_in, x_out, x_in, y_out, y_in, z_out, z_in,
    f_send, f_in, n_c, n_x, n_y, n_zb, n_za,
    load, store,
    ya_s, ya_r, za_s, za_r, yb_s, yb_r, zb_s, zb_r,
    wz_s, wz_r, wy_s, wy_r, wx_s, wx_r, wc_s, wc_r,
    gc_s, gc_r, gx_s, gx_r, gy_s, gy_r, gz_s, gz_r, gf_s, gf_r,
    nc_s, nc_r, nx_s, nx_r, ny_s, ny_r, nzb_s, nzb_r, nza_s, nza_r,
):
    g = lax.axis_index("grp")
    f = lax.axis_index("fsdp")
    core = g % s.c
    my_x = (g // s.c) % s.x
    my_yh = g // (s.c * s.x)
    my_z = f // s.yl
    my_yl = f % s.yl
    my_y = my_yh * s.yl + my_yl
    other = 1 - core

    def grp_of(yh, x, c):
        return (yh * s.x + x) * s.c + c

    def at_z(z):
        return (g, z * s.yl + my_yl)

    def at_yl(yl):
        return (g, my_z * s.yl + yl)

    def at_y(y):
        return (grp_of(y // s.yl, my_x, core), my_z * s.yl + y % s.yl)

    def at_x(x):
        return (grp_of(my_yh, x, core), f)

    sibling = (grp_of(my_yh, my_x, other), f)

    def others(count, me, body):
        def step(i, carry):
            body((me + count // 2 + (i + 1) // 2 * (1 - 2 * (i % 2))) % count)
            return carry

        lax.fori_loop(0, count - 1, step, 0)

    def remote(src, dst, send, recv, device):
        return pltpu.make_async_remote_copy(
            src_ref=src, dst_ref=dst, send_sem=send, recv_sem=recv,
            device_id=device, device_id_type=MESH,
        )

    ends = []

    def rows_of(ref, k, count):
        return ref.at[pl.ds(pl.multiple_of(k * count, count), count), :]

    class Exchange:
        def __init__(self, src, dst, rows, count, me, send, recv, at, spread=True):
            self.src, self.dst, self.rows, self.count, self.me = src, dst, rows, count, me
            self.send, self.recv, self.at, self.spread = send, recv, at, spread

        def copy(self, p):
            block = rows_of(self.src, p if self.spread else 0, self.rows)
            return remote(block, rows_of(self.dst, self.me, self.rows), self.send, self.recv, self.at(p))

        def start(self):
            others(self.count, self.me, lambda p: self.copy(p).start())
            self.started()

        def start_one(self, p):
            @pl.when(p != self.me)
            def _():
                self.copy(p).start()

        def started(self):
            ends.append(self.whole().wait_send)
            mine = rows_of(self.src, self.me if self.spread else 0, self.rows)
            rows_of(self.dst, self.me, self.rows)[...] = mine[...]

        def whole(self):
            part = self.dst.at[pl.ds(0, (self.count - 1) * self.rows), :]
            return remote(part, part, self.send, self.recv, self.at((self.me + 1) % self.count))

        def wait(self):
            self.whole().wait_recv()

    barrier = pltpu.get_barrier_semaphore()

    def greet(device):
        pl.semaphore_signal(barrier, inc=1, device_id=device, device_id_type=MESH)

    others(s.z, my_z, lambda z: greet(at_z(z)))
    others(s.y, my_y, lambda y: greet(at_y(y)))
    others(s.x, my_x, lambda x: greet(at_x(x)))
    greet(sibling)

    inputs = [
        (send_order_h, send_order), (table_h, table), (tok_h, tok), (wshard_h, wshard), (recv_order_h, recv_order),
        (row_ids_h, row_ids), (frames_h, frames), (gains_h, gains), (biases_h, biases), (dout_h, dout),
    ]
    loads = [pltpu.make_async_copy(src, dst, load.at[i]) for i, (src, dst) in enumerate(inputs)]
    for copy in loads:
        copy.start()

    for copy in loads:
        copy.wait()
    to_q = one_hot(s.slots, table[2:3, : s.slots])
    perm[...] = to_q
    pt[...] = one_hot(s.slots, send_order[...])
    pt_q[...] = mm(pt[...], to_q).astype(BF16)
    rt[...] = one_hot(s.slots, recv_order[...])
    rt_q[...] = mm(to_q, rt[...], TN).astype(BF16)
    wpad[...] = jnp.zeros_like(wpad)
    wpad[0 : s.rows, :] = wshard[:, : s.kept]
    for k in range(3 if s.fold else 0):
        down_rows = one_hot(s.rows, table[5 + k : 6 + k, :ROWS16])
        folded = mm(down_rows, wshard[:, s.kept :], TN).astype(BF16)
        wpad[:, k * s.fold : (k + 1) * s.fold] += folded
    for c in range(CHUNKS):
        a_out[c] = mm(pt_q[...], tok[:, c * s.chunk : (c + 1) * s.chunk], TN).astype(BF16)
    pl.semaphore_wait(barrier, (s.z - 1) + (s.y - 1) + (s.x - 1) + 1)

    run = s.slots // s.yl
    block = s.slots // s.z

    def along_yl(out, into, send, recv):
        return [
            Exchange(out.at[c], into.at[c], run, s.yl, my_yl, send.at[c], recv.at[c], at_yl) for c in range(CHUNKS)
        ]

    def along_z(out, into, send, recv):
        return [
            Exchange(out.at[c], into.at[c], block, s.z, my_z, send.at[c], recv.at[c], at_z) for c in range(CHUNKS)
        ]

    first_y = along_yl(a_out, a_in, ya_s, ya_r)
    first_z = along_z(b_out, b_in, za_s, za_r)
    back_y = along_yl(r_out, r_in, yb_s, yb_r)
    back_z = along_z(t_out, t_in, zb_s, zb_r)

    def wz_copy(z):
        return remote(wpad, wsh, wz_s.at[0], wz_r.at[0], at_z(z))

    @pl.when(my_z == g)
    def _():
        others(s.z, my_z, lambda z: wz_copy(z).start())
        wsh[...] = wpad[...]

    first_y[0].start()
    first_y[1].start()

    def first_turn(c):
        first_y[c].wait()
        if c == 0:
            for later in first_y[2:]:
                later.start()
        b_out[c] = mm(perm[...], a_in[c]).astype(BF16)
        first_z[c].start()

    feat[...] = one_hot(s.width, table[0:1, : s.width])
    ids = row_ids[...].astype(F32)
    down = lax.broadcasted_iota(jnp.int32, (s.slots, s.slots), 0)
    across = lax.broadcasted_iota(jnp.int32, (s.slots, s.slots), 1)
    id_col = jnp.sum(jnp.where(down == across, ids, 0.0), axis=1, keepdims=True)
    before = jnp.sum(jnp.where(ids < id_col, 1.0, 0.0), axis=1, keepdims=True)
    place = lax.broadcasted_iota(jnp.int32, (s.slots, 1), 0).astype(F32) - before
    limit = jnp.zeros((s.slots, 1), F32)
    for k in range(frames.shape[1]):
        limit = limit + jnp.where(id_col == k, frames[0:1, k : k + 1].astype(F32), 0.0)
    aud[...] = jnp.where(place >= limit, 1.0, 0.0)
    same[...] = jnp.where(ids == id_col, 1.0, 0.0)

    wide = s.yl * s.rows
    pick = one_hot(wide, table[3:4, : s.yl * ROWS16])

    def w_rows(yh, x, c):
        return rows_of(weight, grp_of(yh, x, c), wide)

    def wx_copy(yh, x, slot):
        rows = w_rows(yh, slot, core)
        return remote(rows, rows, wx_s.at[x * s.yh + yh], wx_r.at[slot * s.yh + yh], at_x(x))

    def wc_copy(yh, x, c):
        rows = w_rows(yh, x, c)
        return remote(rows, rows, wc_s.at[x * s.yh + yh], wc_r.at[x * s.yh + yh], sibling)

    first_turn(0)

    @pl.when(my_z != g)
    def _():
        wz_copy((my_z + 1) % s.z).wait_recv()

    def wy_copy(y):
        slot = rows_of(wyin, my_y, ROWS16)
        return remote(wsh, slot, wy_s.at[0], wy_r.at[my_yh], at_y(y))

    def wy_part(at, count, send, recv):
        part = wyin.at[pl.ds(at, count * ROWS16), :]
        return remote(part, part, send, recv, at_y((my_y + 1) % s.y))

    others(s.y, my_y, lambda y: wy_copy(y).start())
    ends.append(wy_part(0, s.y - 1, wy_s.at[0], wy_r.at[0]).wait_send)
    rows_of(wyin, my_y, ROWS16)[...] = wsh[...]
    first_turn(1)
    first_turn(2)

    run16 = s.yl * ROWS16
    for step in range(s.yh):
        yh = (my_yh + step) % s.yh
        wy_part(0, s.yl - 1 if step == 0 else s.yl, wy_s.at[0], wy_r.at[yh]).wait_recv()
        shards_of = wyin[pl.ds(pl.multiple_of(yh * run16, run16), run16), :]
        w_block = w_rows(yh, my_x, core)
        w_block[:, 0 : s.kept] = mm(pick, shards_of).astype(BF16)
        if s.fold:
            w_block[:, s.kept :] = sum(
                mm(one_hot(wide, table[5 + k : 6 + k, : s.yl * ROWS16]), shards_of[:, k * s.fold : (k + 1) * s.fold])
                for k in range(3)
            ).astype(BF16)
        others(s.x, my_x, lambda x, yh=yh: wx_copy(yh, x, my_x).start())
        wc_copy(yh, my_x, core).start()

    def unpack(c):
        first_z[c].wait()
        packed[:, c * s.chunk : (c + 1) * s.chunk] = mm(rt[...], b_in[c], TN).astype(BF16)

    def pass_on(step):
        yh = (my_yh + step) % s.yh

        def one(x):
            wx_copy(yh, x, x).wait_recv()
            wc_copy(yh, x, core).start()

        others(s.x, my_x, one)

    for c in range(CHUNKS - 1):
        unpack(c)
    for step in range(s.yh - 1):
        pass_on(step)
    unpack(CHUNKS - 1)

    def by_rows(step_rows, body):
        def step(i, carry):
            body(pl.ds(pl.multiple_of(i * step_rows, step_rows), step_rows))
            return carry

        lax.fori_loop(0, s.slots // step_rows, step, 0)

    def norm(rows):
        values = packed[rows, :].astype(F32)
        centered = values - jnp.mean(values, axis=1, keepdims=True)
        variance = jnp.mean(centered * centered, axis=1, keepdims=True)
        inverse = lax.rsqrt(variance + EPSILON)
        unit = centered * inverse
        inv[rows, :] = inverse
        standard[rows, :] = unit
        audio = jnp.broadcast_to(aud[rows, :], unit.shape) > 0.5
        gain = jnp.where(audio, gains[1:2, :], gains[0:1, :])
        bias = jnp.where(audio, biases[1:2, :], biases[0:1, :])
        normed[rows, :] = (unit * gain + bias).astype(BF16)

    by_rows(NORM_ROWS, norm)
    pass_on(s.yh - 1)
    for h in range(2):
        normed_p[h] = mm(normed[...], feat[:, h * s.half : (h + 1) * s.half]).astype(BF16)

    def wc_all(body):
        for x in range(s.x):
            for yh in range(s.yh):
                body(wc_copy(yh, x, other))

    wc_all(lambda copy: copy.wait_recv())

    def project(i, carry):
        cols = pl.ds(pl.multiple_of(i * s.inner, LANES), s.inner)
        qkv[:, cols] = mm(normed[...], weight[:, cols]).astype(BF16)
        return carry

    lax.fori_loop(0, 3, project, 0, unroll=True)

    pair = 2 * HEAD_DIM
    scaling = 1.0 / HEAD_DIM**0.5

    def heads(i, carry):
        def part(k):
            return pl.ds(pl.multiple_of(k * s.inner + i * pair, LANES), pair)

        lane = lax.broadcasted_iota(jnp.int32, (1, pair), 1)
        masks = [jnp.where(lane < HEAD_DIM, 1.0, 0.0), jnp.where(lane < HEAD_DIM, 0.0, 1.0)]
        q, k, v, do = qkv[:, part(0)], qkv[:, part(1)], qkv[:, part(2)], dout[:, part(0)]

        def split(a):
            return [a * m.astype(BF16) for m in masks]

        qs, ks, vs, dos = split(q), split(k), split(v), split(do)
        probs = []
        for a in range(2):
            scores = jnp.where(same[...] > 0.5, mm(qs[a], k, NT) * scaling, -1e30)
            exponent = jnp.exp(scores - jnp.max(scores, axis=1, keepdims=True))
            probs.append((exponent / jnp.sum(exponent, axis=1, keepdims=True)).astype(BF16))
        out = mm(jnp.concatenate(probs, axis=1), jnp.concatenate(vs, axis=0)).astype(BF16)
        attended[:, part(0)] = out
        delta = do.astype(F32) * out.astype(F32)
        grads = []
        for a in range(2):
            row_delta = jnp.sum(delta * masks[a], axis=1, keepdims=True)
            grad_probs = mm(dos[a], v, NT)
            grads.append((probs[a].astype(F32) * (grad_probs - row_delta) * scaling).astype(BF16))
        gqkv[:, part(0)] = mm(
            jnp.concatenate(grads, axis=1), jnp.concatenate(ks, axis=0)
        ).astype(BF16)
        gqkv[:, part(1)] = mm(
            jnp.concatenate(grads, axis=0), jnp.concatenate(qs, axis=0), TN
        ).astype(BF16)
        gqkv[:, part(2)] = mm(
            jnp.concatenate(probs, axis=0), jnp.concatenate(dos, axis=0), TN
        ).astype(BF16)
        return carry

    lax.fori_loop(0, s.inner // pair, heads, 0, unroll=True)
    stores = []

    def keep(src, dst):
        copy = pltpu.make_async_copy(src, dst, store.at[len(stores)])
        copy.start()
        stores.append(copy)

    keep(attended, attended_h)

    third = s.columns // 3

    def third_rows(k):
        return pl.ds(k * third, third)

    def gc_copy(k):
        return remote(g_send.at[third_rows(k), :], g_in.at[third_rows(k), :], gc_s.at[k], gc_r.at[k], sibling)

    for k in range(3):
        g_send[third_rows(k), :] = mm(gqkv[:, k * third : (k + 1) * third], normed_p[other], TN).astype(BF16)
        gc_copy(k).start()
        ends.append(gc_copy(k).wait_send)

    def unproject(i, carry):
        rows = pl.ds(pl.multiple_of(i * s.chunk, s.chunk), s.chunk)
        gnorm[i] = mm(gqkv[...], weight[rows, :], NT)
        return carry

    lax.fori_loop(0, CHUNKS, unproject, 0, unroll=True)
    def piece_rows(p):
        return pl.ds(pl.multiple_of(p * s.chip_block, ROWS16), s.chip_block)

    def gx_copy(yh, x, slot):
        return remote(x_out.at[piece_rows(yh * s.x + x), :], x_in.at[yh, slot], gx_s.at[yh], gx_r.at[yh], at_x(x))

    sent = 0
    for k in range(3):
        g_own[third_rows(k), :] = mm(gqkv[:, k * third : (k + 1) * third], normed_p[core], TN)
        gc_copy(k).wait_recv()
        both = g_own[third_rows(k), :] + g_in[third_rows(k), :].astype(F32)
        g_own[third_rows(k), :] = both
        x_out[third_rows(k), :] = both.astype(BF16)
        while (sent + 1) * s.chip_block <= (k + 1) * third:
            yh, x = sent // s.x, sent % s.x

            @pl.when(x != my_x)
            def _(yh=yh, x=x):
                gx_copy(yh, x, my_x).start()

            sent += 1
    gx_all = []
    for yh in range(s.yh):
        part = x_in.at[yh, pl.ds(0, s.x - 1)]
        gx_all.append(remote(part, part, gx_s.at[yh], gx_r.at[yh], at_x((my_x + 1) % s.x)))
        ends.append(gx_all[yh].wait_send)

    my_za, my_zb = my_z // s.zb, my_z % s.zb
    n_zb[my_zb] = jnp.zeros_like(n_zb[0])

    def unnorm(rows):
        grad = jnp.concatenate([gnorm[c, rows, :] for c in range(CHUNKS)], axis=1)
        unit = standard[rows, :]
        audio = jnp.broadcast_to(aud[rows, :], unit.shape) > 0.5
        gain = jnp.where(audio, gains[1:2, :], gains[0:1, :])
        gain_term = grad * unit
        n_zb[my_zb] += jnp.concatenate(
            [
                jnp.sum(jnp.where(audio, 0.0, gain_term), axis=0, keepdims=True),
                jnp.sum(jnp.where(audio, gain_term, 0.0), axis=0, keepdims=True),
                jnp.sum(jnp.where(audio, 0.0, grad), axis=0, keepdims=True),
                jnp.sum(jnp.where(audio, grad, 0.0), axis=0, keepdims=True),
            ],
            axis=0,
        )
        scaled = grad * gain
        out = inv[rows, :] * (
            scaled
            - jnp.mean(scaled, axis=1, keepdims=True)
            - unit * jnp.mean(scaled * unit, axis=1, keepdims=True)
        )
        gpacked[rows, :] = out.astype(BF16)

    by_rows(UNNORM_ROWS, unnorm)

    def total(buf, count):
        result = buf[0]
        for k in range(1, count):
            result = result + buf[k]
        return result

    class Sum:
        def __init__(self, buf, count, me, send, recv, at):
            self.buf, self.count, self.me, self.at = buf, count, me, at
            self.send, self.recv = send.at[0], recv.at[0]

        def start(self, value=None):
            if value is not None:
                self.buf[self.me] = value
            mine = self.buf.at[self.me]
            others(self.count, self.me, lambda p: remote(mine, mine, self.send, self.recv, self.at(p)).start())
            ends.append(self.whole().wait_send)

        def whole(self):
            part = self.buf.at[pl.ds(0, self.count - 1)]
            return remote(part, part, self.send, self.recv, self.at((self.me + 1) % self.count))

        def result(self):
            self.whole().wait_recv()
            return total(self.buf, self.count)

    sum_zb = Sum(n_zb, s.zb, my_zb, nzb_s, nzb_r, lambda zb: at_z(my_za * s.zb + zb))
    sum_za = Sum(n_za, s.za, my_za, nza_s, nza_r, lambda za: at_z(za * s.zb + my_zb))
    sum_c = Sum(n_c, s.c, core, nc_s, nc_r, lambda c: (grp_of(my_yh, my_x, c), f))
    sum_y = Sum(n_y, s.y, my_y, ny_s, ny_r, at_y)
    sum_x = Sum(n_x, s.x, my_x, nx_s, nx_r, at_x)
    sum_zb.start()

    for c in range(CHUNKS):
        r_out[c] = mm(rt_q[...], gpacked[:, c * s.chunk : (c + 1) * s.chunk]).astype(BF16)
        back_y[c].start()

    def back_turn(c):
        back_y[c].wait()
        t_out[c] = mm(perm[...], r_in[c]).astype(BF16)
        back_z[c].start()

    sum_za.start(sum_zb.result())
    back_turn(0)

    spread = one_hot(s.half, table[1:2, : s.yl * LANES])
    gy = Exchange(y_out, y_in, s.chip_block, s.y, my_y, gy_s.at[0], gy_r.at[0], at_y)
    for yh in range(s.yh):
        gx_all[yh].wait_recv()
        piece = g_own[piece_rows(yh * s.x + my_x), :]
        for step in range(1, s.x):
            piece = piece + x_in[yh, (my_x + step) % s.x].astype(F32)
        wide_piece = mm(piece.astype(BF16), spread).astype(BF16)
        for yl in range(s.yl):
            at = (yh * s.yl + yl) * s.chip_block
            y_out[at : at + s.chip_block, :] = wide_piece[:, yl * LANES : (yl + 1) * LANES]
            gy.start_one(yh * s.yl + yl)
        if yh == 0:
            back_turn(1)
    gy.started()
    back_turn(2)
    sum_c.start(sum_za.result())
    sum_y.start(sum_c.result())

    gy.wait()
    piece = y_in[0 : s.chip_block, :].astype(F32)
    for y in range(1, s.y):
        piece = piece + y_in[y * s.chip_block : (y + 1) * s.chip_block, :].astype(F32)
    apart = one_hot(s.z * ROWS8, table[4:5, :LANES])
    z_out[...] = mm(apart, piece.astype(BF16), NT)
    gz = Exchange(z_out, z_in, ROWS8, s.z, my_z, gz_s.at[0], gz_r.at[0], at_z)
    gz.start()
    sum_x.start(sum_y.result())

    def home(c):
        back_z[c].wait()
        grad_tokens[c] = mm(pt[...], t_in[c]).astype(BF16)
        keep(grad_tokens.at[c], grad_tokens_h.at[:, pl.ds(c * s.chunk, s.chunk)])

    home(0)
    home(1)

    @pl.when(my_z == g)
    def _():
        part = weight.at[pl.ds(0, (s.z - 1) * ROWS16), pl.ds(0, s.kept)]
        remote(part, part, wz_s.at[0], wz_r.at[0], at_z((my_z + 1) % s.z)).wait_send()

    others(s.x, my_x, lambda x: [wx_copy(yh, x, my_x).wait_send() for yh in range(s.yh)])
    wc_all(lambda copy: copy.wait_send())
    for wait in ends[:-2]:
        wait()
    last_ends = ends[-2:]
    del ends[:]
    gz.wait()
    own = z_in[0:ROWS8, :]
    for z in range(1, s.z):
        own = own + z_in[z * ROWS8 : (z + 1) * ROWS8, :]
    f_send[...] = own
    f_copy = remote(f_send, f_in, gf_s.at[0], gf_r.at[0], sibling)
    f_copy.start()
    ends.append(f_copy.wait_send)
    home(2)
    norms = sum_x.result()
    grad_scale[...] = norms[0:2]
    grad_shift[...] = norms[2:4]
    keep(grad_scale, grad_scale_h)
    keep(grad_shift, grad_shift_h)
    f_copy.wait_recv()
    first = core == 0
    theirs = f_in[...]
    low, high = jnp.where(first, own, theirs), jnp.where(first, theirs, own)
    for at, value in ((0, low), (s.half_rows, high)):
        mine = jnp.where(first, value[:, : s.col_block], value[:, s.col_block :])
        grad_weight[at : at + s.half_rows, :] = mine[: s.half_rows]
    keep(grad_weight, grad_weight_h)

    for wait in last_ends + ends:
        wait()
    for copy in stores:
        copy.wait()


def copy_out(*refs):
    count = (len(refs) - 2) // 3
    sources, targets, held = refs[:count], refs[count : 2 * count], refs[2 * count : 3 * count]
    load, store = refs[3 * count :]
    loads = [pltpu.make_async_copy(sources[i], held[i], load.at[i]) for i in range(count)]
    stores = [pltpu.make_async_copy(held[i], targets[i], store.at[i]) for i in range(count)]
    for copy in loads:
        copy.start()
    for i in range(count):
        loads[i].wait()
        stores[i].start()
    for copy in stores:
        copy.wait()


def shards(
    tokens, send_order, recv_order, row_ids, frames, norm_scale, norm_shift, qkv_weight, d_out
):
    slots, width = tokens.shape
    columns = qkv_weight.shape[1]
    s = Sizes(lax.axis_size("grp"), lax.axis_size("fsdp"), slots, width, columns)
    whole = pl.BlockSpec(memory_space=pl.ANY)
    vm, dma = pltpu.VMEM, pltpu.SemaphoreType.DMA
    moved = vm((CHUNKS, slots, s.chunk), BF16)
    norms = (4, width)
    args = (
        tokens, send_order, recv_order, row_ids, frames, norm_scale, norm_shift, qkv_weight, d_out,
        jnp.asarray(index_rows(s)),
    )
    sds = jax.ShapeDtypeStruct
    outs = (
        sds((slots, s.inner), BF16), sds((slots, width), BF16),
        sds((s.rows, s.col_block), F32), sds((2, width), F32), sds((2, width), F32),
    )
    scratch = [vm(a.shape, a.dtype) for a in args]
    scratch += [vm((slots, s.inner), BF16), moved]
    scratch += [vm(a.shape, a.dtype) for a in outs[2:]]
    scratch += [
        vm((slots, slots), BF16), vm((slots, slots), BF16), vm((slots, slots), BF16),
        vm((slots, slots), BF16), vm((slots, slots), BF16),
        vm((width, width), BF16), moved, moved, moved, moved, vm((slots, width), BF16),
        vm((ROWS16, s.kept), BF16), vm((ROWS16, s.kept), BF16),
        vm((s.y * ROWS16, s.kept), BF16), vm((width, columns), BF16),
        vm((slots, 1), F32), vm((slots, slots), F32), vm((slots, width), F32), vm((slots, 1), F32),
        vm((slots, width), BF16), vm((2, slots, s.half), BF16),
        vm((slots, columns), BF16), vm((slots, columns), BF16),
        vm((CHUNKS, slots, s.chunk), F32), vm((slots, width), BF16),
        moved, moved, moved, moved,
        vm((columns, s.half), BF16), vm((columns, s.half), F32), vm((columns, s.half), BF16),
        vm((columns, s.half), BF16), vm((s.yh, s.x, s.chip_block, s.half), BF16),
        vm((s.y * s.chip_block, LANES), BF16), vm((s.y * s.chip_block, LANES), BF16),
        vm((s.z * ROWS8, s.chip_block), F32), vm((s.z * ROWS8, s.chip_block), F32),
        vm((ROWS8, s.chip_block), F32), vm((ROWS8, s.chip_block), F32),
        vm((s.c,) + norms, F32), vm((s.x,) + norms, F32), vm((s.y,) + norms, F32),
        vm((s.zb,) + norms, F32), vm((s.za,) + norms, F32),
    ]
    xy = s.x * s.yh
    counts = [len(args), len(outs) + CHUNKS - 1]
    counts += [CHUNKS] * 8
    counts += [1, 1, 1, s.yh, xy, xy, xy, xy]
    counts += [3, 3, s.yh, s.yh] + [1] * 6
    counts += [1] * 10
    scratch += [dma((n,)) for n in counts]
    results = pl.pallas_call(
        functools.partial(kernel, s),
        out_shape=outs,
        in_specs=[whole] * len(args),
        out_specs=(whole,) * len(outs),
        scratch_shapes=scratch,
        compiler_params=pltpu.CompilerParams(
            collective_id=0, has_side_effects=True, vmem_limit_bytes=56 * 1024 * 1024
        ),
        cost_estimate=pl.CostEstimate(
            flops=2_000_000_000, bytes_accessed=3_000_000, transcendentals=400_000
        ),
        name="joint_block",
    )(*args)
    return pl.pallas_call(
        copy_out,
        out_shape=outs,
        in_specs=[whole] * len(outs),
        out_specs=(whole,) * len(outs),
        scratch_shapes=[vm(a.shape, a.dtype) for a in outs] + [dma((len(outs),))] * 2,
        name="copy_out",
    )(*results)


def solution(mesh):
    rows = P(("grp", "fsdp"), None)
    return jax.shard_map(
        shards,
        mesh=mesh,
        in_specs=(rows, rows, rows, rows, rows, P(), P(), P("fsdp", None), rows),
        out_specs=(rows, rows, P("fsdp", "grp"), P(), P()),
        check_vma=False,
    )
```

time: 120 us -> 97.2 us (0.81); the launches traced: 119 us -> 97 us
  Pallas kernels: 113 us -> 96.4 us
  local copies, waits for them, and re-layouts: 4.41 us -> 0 us
    pallas_call x1 -> x2, Pallas kernels: 113 us -> 96.4 us  [the longest x1 94.4 us: shards(): pl.pallas_call(functools.partial(kernel, s), out_shape=outs, in_specs=[wh...]
    unnamed x13 -> x0, local copies, waits for them, and re-layouts: 4.41 us -> none
where the time goes in v2:
time: 97.2 us; the launch traced here: 97 us
  Pallas kernels  96.4 us (99%)
    pallas_call x1, Pallas kernels, shards(): pl.pallas_call(functools.partial(kernel, s), out_shape=outs, in_specs=[wh...  94.4 us

profile of v2, /device:TPU:1, one launch (start us, length us, event | category | flops | bytes accessed | tf_op | source)
XLA Modules:
  0.0 97.0 jit_solution(3344991418164155218)
XLA Ops:
  0.6 94.4 %joint_block.1 = (bf16[256,384]{1,0:T(8,128)(2,1)}, bf16[256,768]{1,0:T(8,128)(2,1)}, f32[12,72]{1,0:T(8,128)}, f32[2,768]{1,0:T(2,128)}, f32[2,768]{1,0:T(2,128)}) custom-call(bf16[256,768]{1,0:T(8,128)(2,1)} %tok_h.1, s32[1,256]{1,0:T(1,128)} %send_order_h.1, s32[1,256]{1,0:T(1,128)} %recv_order_h.1, s32[1,256]{1,0:T(1,128)} %row_ids_h.1, ...), custom_call_target="tpu_custom_call" | custom-call | flops 2000000000 | bytes 3000000 | tf_op jit(solution)/shard_map/joint_block/pallas_call | solution.py:676
  95.1 1.9 %copy_out.1 = (bf16[256,384]{1,0:T(8,128)(2,1)}, bf16[256,768]{1,0:T(8,128)(2,1)}, f32[12,72]{1,0:T(8,128)}, f32[2,768]{1,0:T(2,128)}, f32[2,768]{1,0:T(2,128)}) custom-call(bf16[256,384]{1,0:T(8,128)(2,1)} %get-tuple-element.10.refs_0_, bf16[256,768]{1,0:T(8,128)(2,1)} %get-tuple-element.11.refs_1_, f32[12,72]{1,0:T(8,128)} %get-tuple-element.12.refs_2_, ...), custom_call_target="tpu_custom_call" | custom-call | tf_op jit(solution)/shard_map/copy_out/pallas_call | solution.py:690

commit v3 on v2

--- a/solution.py
+++ b/solution.py
@@ -16,7 +16,10 @@
 ROWS16 = 16
 ROWS8 = 8
 LANES = 128
-CHUNKS = 3
+THERE = (1, 2, 2, 1)
+BACK = (2, 2, 1, 1)
+Y_FIRST = (False, True, True, True)
+CHUNKS = len(Y_FIRST)
 NORM_ROWS = 64
 UNNORM_ROWS = 64
 
@@ -37,7 +40,11 @@
         self.col_block = columns // grp
         self.chip_block = self.col_block * self.c
         self.pieces = self.yh * self.x
-        self.chunk = width // CHUNKS
+        sixth = width // 6
+        self.cols, self.back_cols = (
+            [slice(sixth * sum(parts[:c]), sixth * sum(parts[: c + 1])) for c in range(CHUNKS)]
+            for parts in (THERE, BACK)
+        )
         self.half = width // 2
         self.z_lanes = self.z * self.half_rows
         self.fold = (columns // LANES * 2 // 9) * LANES
@@ -205,26 +212,24 @@
         folded = mm(down_rows, wshard[:, s.kept :], TN).astype(BF16)
         wpad[:, k * s.fold : (k + 1) * s.fold] += folded
     for c in range(CHUNKS):
-        a_out[c] = mm(pt_q[...], tok[:, c * s.chunk : (c + 1) * s.chunk], TN).astype(BF16)
+        a_out[c][...] = mm((pt_q if Y_FIRST[c] else pt)[...], tok[:, s.cols[c]], TN).astype(BF16)
     pl.semaphore_wait(barrier, (s.z - 1) + (s.y - 1) + (s.x - 1) + 1)
 
     run = s.slots // s.yl
     block = s.slots // s.z
 
-    def along_yl(out, into, send, recv):
-        return [
-            Exchange(out.at[c], into.at[c], run, s.yl, my_yl, send.at[c], recv.at[c], at_yl) for c in range(CHUNKS)
-        ]
-
-    def along_z(out, into, send, recv):
-        return [
-            Exchange(out.at[c], into.at[c], block, s.z, my_z, send.at[c], recv.at[c], at_z) for c in range(CHUNKS)
-        ]
-
-    first_y = along_yl(a_out, a_in, ya_s, ya_r)
-    first_z = along_z(b_out, b_in, za_s, za_r)
-    back_y = along_yl(r_out, r_in, yb_s, yb_r)
-    back_z = along_z(t_out, t_in, zb_s, zb_r)
+    def along(y, out, into, send, recv, c):
+        if y:
+            return Exchange(out[c], into[c], run, s.yl, my_yl, send.at[c], recv.at[c], at_yl)
+        return Exchange(out[c], into[c], block, s.z, my_z, send.at[c], recv.at[c], at_z)
+
+    def turned(c, value):
+        return mm(perm[...], value, ((1,), (0,)) if Y_FIRST[c] else TN).astype(BF16)
+
+    first_1 = [along(Y_FIRST[c], a_out, a_in, ya_s, ya_r, c) for c in range(CHUNKS)]
+    first_2 = [along(not Y_FIRST[c], b_out, b_in, za_s, za_r, c) for c in range(CHUNKS)]
+    back_1 = [along(Y_FIRST[c], r_out, r_in, yb_s, yb_r, c) for c in range(CHUNKS)]
+    back_2 = [along(not Y_FIRST[c], t_out, t_in, zb_s, zb_r, c) for c in range(CHUNKS)]
 
     def wz_copy(z):
         return remote(wpad, wsh, wz_s.at[0], wz_r.at[0], at_z(z))
@@ -234,16 +239,13 @@
         others(s.z, my_z, lambda z: wz_copy(z).start())
         wsh[...] = wpad[...]
 
-    first_y[0].start()
-    first_y[1].start()
+    for c in range(CHUNKS):
+        first_1[c].start()
 
     def first_turn(c):
-        first_y[c].wait()
-        if c == 0:
-            for later in first_y[2:]:
-                later.start()
-        b_out[c] = mm(perm[...], a_in[c]).astype(BF16)
-        first_z[c].start()
+        first_1[c].wait()
+        b_out[c][...] = turned(c, a_in[c][...])
+        first_2[c].start()
 
     feat[...] = one_hot(s.width, table[0:1, : s.width])
     ids = row_ids[...].astype(F32)
@@ -256,7 +258,7 @@
     for k in range(frames.shape[1]):
         limit = limit + jnp.where(id_col == k, frames[0:1, k : k + 1].astype(F32), 0.0)
     aud[...] = jnp.where(place >= limit, 1.0, 0.0)
-    same[...] = jnp.where(ids == id_col, 1.0, 0.0)
+    same[...] = jnp.where(ids == id_col, 0.0, -1e30)
 
     wide = s.yl * s.rows
     pick = one_hot(wide, table[3:4, : s.yl * ROWS16])
@@ -272,8 +274,6 @@
         rows = w_rows(yh, x, c)
         return remote(rows, rows, wc_s.at[x * s.yh + yh], wc_r.at[x * s.yh + yh], sibling)
 
-    first_turn(0)
-
     @pl.when(my_z != g)
     def _():
         wz_copy((my_z + 1) % s.z).wait_recv()
@@ -289,8 +289,8 @@
     others(s.y, my_y, lambda y: wy_copy(y).start())
     ends.append(wy_part(0, s.y - 1, wy_s.at[0], wy_r.at[0]).wait_send)
     rows_of(wyin, my_y, ROWS16)[...] = wsh[...]
-    first_turn(1)
-    first_turn(2)
+    for c in range(1, CHUNKS):
+        first_turn(c)
 
     run16 = s.yl * ROWS16
     for step in range(s.yh):
@@ -307,9 +307,12 @@
         others(s.x, my_x, lambda x, yh=yh: wx_copy(yh, x, my_x).start())
         wc_copy(yh, my_x, core).start()
 
+    first_turn(0)
+
     def unpack(c):
-        first_z[c].wait()
-        packed[:, c * s.chunk : (c + 1) * s.chunk] = mm(rt[...], b_in[c], TN).astype(BF16)
+        first_2[c].wait()
+        place_in = rt if Y_FIRST[c] else rt_q
+        packed[:, s.cols[c]] = mm(place_in[...], b_in[c][...], TN).astype(BF16)
 
     def pass_on(step):
         yh = (my_yh + step) % s.yh
@@ -320,11 +323,12 @@
 
         others(s.x, my_x, one)
 
-    for c in range(CHUNKS - 1):
-        unpack(c)
+    unpack(0)
+    unpack(1)
     for step in range(s.yh - 1):
         pass_on(step)
-    unpack(CHUNKS - 1)
+    unpack(2)
+    unpack(3)
 
     def by_rows(step_rows, body):
         def step(i, carry):
@@ -382,9 +386,9 @@
         qs, ks, vs, dos = split(q), split(k), split(v), split(do)
         probs = []
         for a in range(2):
-            scores = jnp.where(same[...] > 0.5, mm(qs[a], k, NT) * scaling, -1e30)
+            scores = mm(qs[a], k, NT) * scaling + same[...]
             exponent = jnp.exp(scores - jnp.max(scores, axis=1, keepdims=True))
-            probs.append((exponent / jnp.sum(exponent, axis=1, keepdims=True)).astype(BF16))
+            probs.append((exponent * (1.0 / jnp.sum(exponent, axis=1, keepdims=True))).astype(BF16))
         out = mm(jnp.concatenate(probs, axis=1), jnp.concatenate(vs, axis=0)).astype(BF16)
         attended[:, part(0)] = out
         delta = do.astype(F32) * out.astype(F32)
@@ -427,12 +431,9 @@
         gc_copy(k).start()
         ends.append(gc_copy(k).wait_send)
 
-    def unproject(i, carry):
-        rows = pl.ds(pl.multiple_of(i * s.chunk, s.chunk), s.chunk)
-        gnorm[i] = mm(gqkv[...], weight[rows, :], NT)
-        return carry
-
-    lax.fori_loop(0, CHUNKS, unproject, 0, unroll=True)
+    for k in range(3):
+        rows = slice(k * s.width // 3, (k + 1) * s.width // 3)
+        gnorm[:, rows] = mm(gqkv[...], weight[rows, :], NT)
     def piece_rows(p):
         return pl.ds(pl.multiple_of(p * s.chip_block, ROWS16), s.chip_block)
 
@@ -464,7 +465,7 @@
     n_zb[my_zb] = jnp.zeros_like(n_zb[0])
 
     def unnorm(rows):
-        grad = jnp.concatenate([gnorm[c, rows, :] for c in range(CHUNKS)], axis=1)
+        grad = gnorm[rows, :]
         unit = standard[rows, :]
         audio = jnp.broadcast_to(aud[rows, :], unit.shape) > 0.5
         gain = jnp.where(audio, gains[1:2, :], gains[0:1, :])
@@ -521,17 +522,22 @@
     sum_x = Sum(n_x, s.x, my_x, nx_s, nx_r, at_x)
     sum_zb.start()
 
-    for c in range(CHUNKS):
-        r_out[c] = mm(rt_q[...], gpacked[:, c * s.chunk : (c + 1) * s.chunk]).astype(BF16)
-        back_y[c].start()
+    for c in (1, 0, 2, 3):
+        place_in = rt_q if Y_FIRST[c] else rt
+        r_out[c][...] = mm(place_in[...], gpacked[:, s.back_cols[c]]).astype(BF16)
+        if c < 2:
+            back_1[c].start()
 
     def back_turn(c):
-        back_y[c].wait()
-        t_out[c] = mm(perm[...], r_in[c]).astype(BF16)
-        back_z[c].start()
-
-    sum_za.start(sum_zb.result())
-    back_turn(0)
+        back_1[c].wait()
+        t_out[c][...] = turned(c, r_in[c][...])
+        back_2[c].start()
+
+    sum_c.start(sum_zb.result())
+    back_turn(1)
+    back_1[2].start()
+    back_1[3].start()
+    sum_x.start(sum_c.result())
 
     spread = one_hot(s.half, table[1:2, : s.yl * LANES])
     gy = Exchange(y_out, y_in, s.chip_block, s.y, my_y, gy_s.at[0], gy_r.at[0], at_y)
@@ -546,11 +552,11 @@
             y_out[at : at + s.chip_block, :] = wide_piece[:, yl * LANES : (yl + 1) * LANES]
             gy.start_one(yh * s.yl + yl)
         if yh == 0:
-            back_turn(1)
+            back_turn(2)
     gy.started()
-    back_turn(2)
-    sum_c.start(sum_za.result())
-    sum_y.start(sum_c.result())
+    sum_za.start(sum_x.result())
+    back_turn(3)
+    back_turn(0)
 
     gy.wait()
     piece = y_in[0 : s.chip_block, :].astype(F32)
@@ -560,15 +566,17 @@
     z_out[...] = mm(apart, piece.astype(BF16), NT)
     gz = Exchange(z_out, z_in, ROWS8, s.z, my_z, gz_s.at[0], gz_r.at[0], at_z)
     gz.start()
-    sum_x.start(sum_y.result())
+    sum_y.start(sum_za.result())
 
     def home(c):
-        back_z[c].wait()
-        grad_tokens[c] = mm(pt[...], t_in[c]).astype(BF16)
-        keep(grad_tokens.at[c], grad_tokens_h.at[:, pl.ds(c * s.chunk, s.chunk)])
+        back_2[c].wait()
+        grad_tokens[c][...] = mm((pt if Y_FIRST[c] else pt_q)[...], t_in[c][...]).astype(BF16)
+        cols = s.back_cols[c]
+        keep(grad_tokens[c], grad_tokens_h.at[:, pl.ds(cols.start, cols.stop - cols.start)])
 
     home(0)
     home(1)
+    home(2)
 
     @pl.when(my_z == g)
     def _():
@@ -589,8 +597,8 @@
     f_copy = remote(f_send, f_in, gf_s.at[0], gf_r.at[0], sibling)
     f_copy.start()
     ends.append(f_copy.wait_send)
-    home(2)
-    norms = sum_x.result()
+    home(3)
+    norms = sum_y.result()
     grad_scale[...] = norms[0:2]
     grad_shift[...] = norms[2:4]
     keep(grad_scale, grad_scale_h)
@@ -633,7 +641,9 @@
     s = Sizes(lax.axis_size("grp"), lax.axis_size("fsdp"), slots, width, columns)
     whole = pl.BlockSpec(memory_space=pl.ANY)
     vm, dma = pltpu.VMEM, pltpu.SemaphoreType.DMA
-    moved = vm((CHUNKS, slots, s.chunk), BF16)
+    there, back = (
+        [vm((slots, cols.stop - cols.start), BF16) for cols in parts] for parts in (s.cols, s.back_cols)
+    )
     norms = (4, width)
     args = (
         tokens, send_order, recv_order, row_ids, frames, norm_scale, norm_shift, qkv_weight, d_out,
@@ -645,19 +655,19 @@
         sds((s.rows, s.col_block), F32), sds((2, width), F32), sds((2, width), F32),
     )
     scratch = [vm(a.shape, a.dtype) for a in args]
-    scratch += [vm((slots, s.inner), BF16), moved]
+    scratch += [vm((slots, s.inner), BF16), back]
     scratch += [vm(a.shape, a.dtype) for a in outs[2:]]
     scratch += [
         vm((slots, slots), BF16), vm((slots, slots), BF16), vm((slots, slots), BF16),
         vm((slots, slots), BF16), vm((slots, slots), BF16),
-        vm((width, width), BF16), moved, moved, moved, moved, vm((slots, width), BF16),
+        vm((width, width), BF16), there, there, there, there, vm((slots, width), BF16),
         vm((ROWS16, s.kept), BF16), vm((ROWS16, s.kept), BF16),
         vm((s.y * ROWS16, s.kept), BF16), vm((width, columns), BF16),
         vm((slots, 1), F32), vm((slots, slots), F32), vm((slots, width), F32), vm((slots, 1), F32),
         vm((slots, width), BF16), vm((2, slots, s.half), BF16),
         vm((slots, columns), BF16), vm((slots, columns), BF16),
-        vm((CHUNKS, slots, s.chunk), F32), vm((slots, width), BF16),
-        moved, moved, moved, moved,
+        vm((slots, width), F32), vm((slots, width), BF16),
+        back, back, back, back,
         vm((columns, s.half), BF16), vm((columns, s.half), F32), vm((columns, s.half), BF16),
         vm((columns, s.half), BF16), vm((s.yh, s.x, s.chip_block, s.half), BF16),
         vm((s.y * s.chip_block, LANES), BF16), vm((s.y * s.chip_block, LANES), BF16),

time: 97.2 us -> 92.6 us (0.953); the launches traced: 97 us -> 90.8 us
  Pallas kernels: 96.4 us -> 90.1 us
    pallas_call x1, Pallas kernels: 94.4 us -> 88.2 us  [shards(): pl.pallas_call(functools.partial(kernel, s), out_shape=outs, in_specs=[wh...]
where the time goes in v3:
time: 92.6 us; the launch traced here: 90.8 us
  Pallas kernels  90.1 us (97%)
    pallas_call x1, Pallas kernels, shards(): pl.pallas_call(functools.partial(kernel, s), out_shape=outs, in_specs=[wh...  88.2 us
    pallas_call x1, Pallas kernels, shards(): pl.pallas_call(copy_out, out_shape=outs, in_specs=[whole] * len(outs), ou...  1.94 us

profile of v3, /device:TPU:1, one launch (start us, length us, event | category | flops | bytes accessed | tf_op | source)
XLA Modules:
  0.0 90.8 jit_solution(9603595506205538711)
XLA Ops:
  0.6 88.2 %joint_block.1 = (bf16[256,384]{1,0:T(8,128)(2,1)}, bf16[256,768]{1,0:T(8,128)(2,1)}, f32[12,72]{1,0:T(8,128)}, f32[2,768]{1,0:T(2,128)}, f32[2,768]{1,0:T(2,128)}) custom-call(bf16[256,768]{1,0:T(8,128)(2,1)} %tok_h.1, s32[1,256]{1,0:T(1,128)} %send_order_h.1, s32[1,256]{1,0:T(1,128)} %recv_order_h.1, s32[1,256]{1,0:T(1,128)} %row_ids_h.1, ...), custom_call_target="tpu_custom_call" | custom-call | flops 2000000000 | bytes 3000000 | tf_op jit(solution)/shard_map/joint_block/pallas_call | solution.py:686
  88.8 1.9 %copy_out.1 = (bf16[256,384]{1,0:T(8,128)(2,1)}, bf16[256,768]{1,0:T(8,128)(2,1)}, f32[12,72]{1,0:T(8,128)}, f32[2,768]{1,0:T(2,128)}, f32[2,768]{1,0:T(2,128)}) custom-call(bf16[256,384]{1,0:T(8,128)(2,1)} %get-tuple-element.10.refs_0_, bf16[256,768]{1,0:T(8,128)(2,1)} %get-tuple-element.11.refs_1_, f32[12,72]{1,0:T(8,128)} %get-tuple-element.12.refs_2_, ...), custom_call_target="tpu_custom_call" | custom-call | tf_op jit(solution)/shard_map/copy_out/pallas_call | solution.py:700

commit v4 on v3

--- a/solution.py
+++ b/solution.py
@@ -323,11 +323,12 @@
 
         others(s.x, my_x, one)
 
-    unpack(0)
     unpack(1)
     for step in range(s.yh - 1):
         pass_on(step)
+    unpack(0)
     unpack(2)
+    pass_on(s.yh - 1)
     unpack(3)
 
     def by_rows(step_rows, body):
@@ -351,7 +352,6 @@
         normed[rows, :] = (unit * gain + bias).astype(BF16)
 
     by_rows(NORM_ROWS, norm)
-    pass_on(s.yh - 1)
     for h in range(2):
         normed_p[h] = mm(normed[...], feat[:, h * s.half : (h + 1) * s.half]).astype(BF16)
 
@@ -551,9 +551,8 @@
             at = (yh * s.yl + yl) * s.chip_block
             y_out[at : at + s.chip_block, :] = wide_piece[:, yl * LANES : (yl + 1) * LANES]
             gy.start_one(yh * s.yl + yl)
-        if yh == 0:
-            back_turn(2)
     gy.started()
+    back_turn(2)
     sum_za.start(sum_x.result())
     back_turn(3)
     back_turn(0)

time: 92.6 us -> 93 us (level); the launches traced: 90.8 us -> 92.6 us
  Pallas kernels: 90.1 us -> 92 us
    pallas_call x1, Pallas kernels: 88.2 us -> 90 us  [shards(): pl.pallas_call(functools.partial(kernel, s), out_shape=outs, in_specs=[wh...]
where the time goes in v4:
time: 93 us; the launch traced here: 92.6 us
  Pallas kernels  92 us (99%)
    pallas_call x1, Pallas kernels, shards(): pl.pallas_call(functools.partial(kernel, s), out_shape=outs, in_specs=[wh...  90 us
    pallas_call x1, Pallas kernels, shards(): pl.pallas_call(copy_out, out_shape=outs, in_specs=[whole] * len(outs), ou...  1.94 us

profile of v4, /device:TPU:1, one launch (start us, length us, event | category | flops | bytes accessed | tf_op | source)
XLA Modules:
  0.0 92.6 jit_solution(16009514112068615865)
XLA Ops:
  0.6 90.0 %joint_block.1 = (bf16[256,384]{1,0:T(8,128)(2,1)}, bf16[256,768]{1,0:T(8,128)(2,1)}, f32[12,72]{1,0:T(8,128)}, f32[2,768]{1,0:T(2,128)}, f32[2,768]{1,0:T(2,128)}) custom-call(bf16[256,768]{1,0:T(8,128)(2,1)} %tok_h.1, s32[1,256]{1,0:T(1,128)} %send_order_h.1, s32[1,256]{1,0:T(1,128)} %recv_order_h.1, s32[1,256]{1,0:T(1,128)} %row_ids_h.1, ...), custom_call_target="tpu_custom_call" | custom-call | flops 2000000000 | bytes 3000000 | tf_op jit(solution)/shard_map/joint_block/pallas_call | solution.py:685
  90.7 1.9 %copy_out.1 = (bf16[256,384]{1,0:T(8,128)(2,1)}, bf16[256,768]{1,0:T(8,128)(2,1)}, f32[12,72]{1,0:T(8,128)}, f32[2,768]{1,0:T(2,128)}, f32[2,768]{1,0:T(2,128)}) custom-call(bf16[256,384]{1,0:T(8,128)(2,1)} %get-tuple-element.10.refs_0_, bf16[256,768]{1,0:T(8,128)(2,1)} %get-tuple-element.11.refs_1_, f32[12,72]{1,0:T(8,128)} %get-tuple-element.12.refs_2_, ...), custom_call_target="tpu_custom_call" | custom-call | tf_op jit(solution)/shard_map/copy_out/pallas_call | solution.py:699
